TPU v7x, 256 devices: a whole 4x4x8 slice. The times are simulated.
256 devices in a mesh: member: 32 (over z_hi, x, y), lat: 2 (over core), lon: 4 (over z_lo).
Axes of the slice: x: 4, y: 4, z: 8 (z_hi: 2, z_lo: 4; z = z_hi * 4 + z_lo), core: 2. Of those that a mesh axis runs over, the one named last changes fastest.
Arguments:
- theta: float32 [128, 256, 1536], P('member', 'lat', 'lon'), may hold values from -6 to 6
- tracer: float32 [2, 256, 1536], P(None, 'lat', 'lon'), may hold values from -6 to 6
- velocity: float32 [2, 2, 256, 1536], P(None, None, 'lat', 'lon'), may hold values from -0.2 to 0.2
- obs_index: int32 [6144], P(('lat', 'lon')), may hold values from 0 to 49151
- observed: float32 [6144], P(('lat', 'lon')), may hold values from -6 to 6
- noise_var: float32 [6144], P(('lat', 'lon')), may hold values from 0.1 to 1
- obs_perturb: float32 [6144, 128], P(('lat', 'lon'), 'member'), may hold values from -6 to 6
Outputs:
- theta_new: float32 [128, 256, 1536], P('member', 'lat', 'lon')
- predicted: float32 [6144, 128], P(('lat', 'lon'), 'member')
Inputs may be any that keep to these rules, and one draw needn't show every extreme that they name: obs_index[o] is a row-major flat cell index within the 128 x 384 tile of block o // 768, blocks numbered latitude-major; stations may share a cell.
All inputs are finite; a program needn't handle non-finite values.
Results may differ from a plain program's by a relative error of at most 0.0003.
Values sent between devices are 32-bit elements; how exact they have to be, the bound alone decides.
A program may use at most 128 MiB of HBM per device.

v0:
```python
import jax
import jax.numpy as jnp
from jax import lax
from jax.sharding import PartitionSpec as P

STEPS = 2
LM = 1


def padded(cells, sides, width, closed):
    for axis, dim in sides:
        count = lax.axis_size(axis)
        ends = count if closed else count - 1
        head = lax.slice_in_dim(cells, 0, width, axis=dim)
        tail = lax.slice_in_dim(cells, cells.shape[dim] - width, cells.shape[dim], axis=dim)
        cells = jnp.concatenate(
            [
                lax.ppermute(tail, axis, [(i, (i + 1) % count) for i in range(ends)]),
                cells,
                lax.ppermute(head, axis, [((i + 1) % count, i) for i in range(ends)]),
            ],
            axis=dim,
        )
    return cells


def rims(field):
    lat_padded = padded(field, (("lat", 2),), 1, False)
    lon_padded = padded(field, (("lon", 3),), 1, True)
    return (
        lat_padded[:, :, :-2],
        lat_padded[:, :, 2:],
        lon_padded[:, :, :, :-2],
        lon_padded[:, :, :, 2:],
    )


def advance(c, kap, velocity, sides, k_sides):
    c_s, c_n, c_w, c_e = sides
    k_s, k_n, k_w, k_e = k_sides
    u = velocity[0][None]
    v = velocity[1][None]
    adv = -(jnp.maximum(u, 0.0) * (c - c_w) + jnp.minimum(u, 0.0) * (c_e - c))
    adv = adv - (jnp.maximum(v, 0.0) * (c - c_s) + jnp.minimum(v, 0.0) * (c_n - c))
    diff = 0.5 * (
        (kap + k_w) * (c_w - c)
        + (kap + k_e) * (c_e - c)
        + (kap + k_s) * (c_s - c)
        + (kap + k_n) * (c_n - c)
    )
    return c + adv + diff + 0.2 * (c[:, ::-1] - c)


def on_device(theta, tracer, velocity, obs_index, observed, noise_var, obs_perturb):
    mem_local, lat_rows, lon_cols = theta.shape
    kap = (0.1 * jax.nn.sigmoid(theta))[:, None]
    c = jnp.broadcast_to(tracer[None], (mem_local, 2, lat_rows, lon_cols))
    k_sides = None
    for step in range(STEPS):
        if step == 0:
            sides = rims(jnp.concatenate([c, kap], axis=1))
            k_sides = tuple((side[:, 2:] for side in sides))
            sides = tuple((side[:, :2] for side in sides))
        else:
            sides = rims(c)
        c = advance(c, kap, velocity, sides, k_sides)
    own_pred = jnp.take(c[:, 0].reshape(mem_local, -1), obs_index, axis=1).T
    all_pred = lax.all_gather(own_pred, "member", axis=1, tiled=True)
    members = all_pred.shape[1]
    scale = 1.0 / jnp.sqrt(jnp.float32(members - 1))
    anom_g = (all_pred - jnp.mean(all_pred, axis=1, keepdims=True)) * scale
    weighted = anom_g / noise_var[:, None]
    innov = observed[:, None] + jnp.sqrt(noise_var)[:, None] * obs_perturb - own_pred
    rhs_local = jnp.dot(weighted.T, innov, precision=lax.Precision.HIGHEST)
    gram_part = jnp.dot(weighted.T, anom_g, precision=lax.Precision.HIGHEST)
    gram, rhs_local = lax.psum((gram_part, rhs_local), ("lat", "lon"))
    damped = gram + LM * jnp.eye(members, dtype=gram.dtype)
    factor = jnp.linalg.cholesky(damped)
    half = lax.linalg.triangular_solve(factor, rhs_local, left_side=True, lower=True)
    w_local = lax.linalg.triangular_solve(
        factor, half, left_side=True, lower=True, transpose_a=True
    )
    piece = lax.all_gather(theta, "member", axis=0, tiled=True)
    count = piece.shape[0]
    flat_piece = piece.reshape(count, -1)
    acc = jnp.dot(w_local.T, flat_piece, precision=lax.Precision.HIGHEST)
    acc, total = (acc, jnp.sum(flat_piece, axis=0))
    mean_field = total / members
    update = scale * (acc - jnp.sum(w_local, axis=0)[:, None] * mean_field[None])
    theta_new = theta + update.reshape(theta.shape)
    return (theta_new, own_pred)


def solution(mesh):
    placed = (
        P("member", "lat", "lon"),
        P(None, "lat", "lon"),
        P(None, None, "lat", "lon"),
        P(("lat", "lon")),
        P(("lat", "lon")),
        P(("lat", "lon")),
        P(("lat", "lon"), "member"),
    )
    return jax.shard_map(
        on_device,
        mesh=mesh,
        in_specs=placed,
        out_specs=(P("member", "lat", "lon"), P(("lat", "lon"), "member")),
        check_vma=False,
    )
```

profile of v0, /device:TPU:1, one launch (start us, length us, event | category | flops | bytes accessed | tf_op | source)
XLA Modules:
  0.0 605.3 jit_solution(4109070299127897652)
XLA Ops:
  8.1 1.4 multiply_bitcast_fusion
  9.6 1.2 fusion.11
  10.7 2.0 copy.56
  12.7 2.5 collective-permute-start
  16.0 2.7 collective-permute-start.1
  19.4 1.3 collective-permute-start.2
  21.3 5.0 collective-permute-start.3
  26.3 1.0 maximum_bitcast_fusion.1
  27.4 1.0 copy.57
  28.3 1.9 copy.59
  30.2 2.3 maximum_maximum_fusion
  36.8 1.8 multiply_add_fusion
  38.6 1.2 fusion.52
  39.9 3.2 collective-permute-start.5
  43.7 1.3 collective-permute-start.6
  45.6 4.2 collective-permute-start.7
  51.2 1.3 rev.7
  54.0 1.6 collective-permute-done.4
  55.6 8.8 %collective-permute-done.5 = f32[4,2,128,1]{3,2,0,1:T(8,128)} collective-permute-done((f32[4,2,128,1]{3,2,0,1:T(8,128)}, f32[4,2,128,1]{3,2,0,1:T(8,128)}, u32[]{:S(2)}, u32[]{:S(2)}) %collective-permute-start.5) | collective-permute-done | bytes 4128 | tf_op jit(solution)/shard_map/ppermute | solution.py:20
  64.4 3.0 fusion.8
  68.1 12.8 %copy.71 = f32[4,1,128,384]{0,3,2,1:T(8,128)} copy(f32[4,1,128,384]{3,2,0,1:T(8,128)S(1)} %fusion.14) | data formatting | bytes 1572864 | tf_op jit(solution)/shard_map/reshape;squeeze | solution.py:67
  80.9 9.7 %gather_fusion = f32[768,4]{1,0:T(8,128)S(1)} fusion(f32[4,49152]{0,1:T(8,128)} %bitcast.47, s32[1024]{0:T(1024)S(1)} %pad_clamp_fusion), kind=kCustom, calls=%fused_computation | custom fusion | bytes 27648 | tf_op jit(solution)/shard_map/jit(_take)/gather | solution.py:67
  90.8 104.8 %all-gather = f32[32,4,768]{2,1,0:T(4,128)S(1)} all-gather(f32[1,4,768]{2,1,0:T(4,128)S(1)} %fusion.58), channel_id=1, replica_groups=mesh['member'=32,'lat'=2,'lon'=4] {'member'}, dimensions={0}, use_global_device_ids=true | all-gather | bytes 405504 | tf_op jit(solution)/shard_map/all_gather | solution.py:68
  195.9 1.2 fusion.27
  198.1 29.4 %psum.15 = f32[128,4]{0,1:T(4,128)S(1)} all-reduce(f32[128,4]{0,1:T(4,128)S(1)} %fusion.29), channel_id=1, replica_groups=mesh['member'=32,'lat'=2,'lon'=4] {'lat','lon'}, use_global_device_ids=true, to_apply=%region_4.5 | all-reduce | flops 512 | bytes 4096 | tf_op jit(solution)/shard_map/psum | solution.py:76
  227.5 95.7 %all-reduce.2.cloned.1.call-done = f32[128,128]{1,0:T(8,128)} async-done(((f32[128,128]{1,0:T(8,128)}), f32[128,128]{1,0:T(8,128)}) %all-reduce.2.cloned.1.call-update) | async-done | bytes 65552 | tf_op jit(solution)/shard_map/psum | solution.py:76
  325.0 11.7 %cholesky.17 = f32[128,128]{1,0:T(8,128)S(1)} custom-call(f32[128,128]{1,0:T(8,128)S(1)} %fusion.42), custom_call_target="Cholesky" | custom-call | tf_op jit(solution)/shard_map/jit(cholesky)/cholesky | solution.py:78
  338.1 9.8 %custom-call.8 = f32[1,128,128]{1,2,0:T(8,128)S(1)} custom-call(f32[1,128,128]{2,1,0:T(8,128)S(1)} %fusion.37), custom_call_target="InvertDiagBlocksLowerTriangular" | custom-call | tf_op jit(solution)/shard_map/triangular_solve | solution.py:80
  348.4 197.1 %all-gather.3.cloned.1.call-done = f32[128,128,384]{2,1,0:T(8,128)} async-done(((f32[4,128,384]{2,1,0:T(8,128)}), f32[128,128,384]{2,1,0:T(8,128)}) %all-gather.3.cloned.1.call-update) | async-done | bytes 25165840 | tf_op jit(solution)/shard_map/all_gather | solution.py:83
  545.5 26.8 %copy.72 = f32[16,8,128,384]{3,1,2,0:T(8,128)} copy(f32[16,8,128,384]{3,2,1,0:T(8,128)} %bitcast.45) | data formatting | bytes 50331648
  572.3 9.3 %reduce_sum.29 = f32[128,384]{1,0:T(8,128)S(1)} reduce(f32[128,128,384]{2,1,0:T(8,128)} %all-gather.3.cloned.1.call-done, f32[]{:T(128)} %constant.68.clone.1), dimensions={0}, to_apply=%region_6.7 | reduce | flops 6242304 | bytes 25362436 | tf_op jit(solution)/shard_map/reduce_sum | solution.py:87
  581.6 15.2 %fusion = f32[4,49152]{1,0:T(4,128)S(1)} fusion(f32[128,4]{0,1:T(4,128)S(1)} %get-tuple-element.43, f32[128,49152]{1,0:T(8,128)} %bitcast.46, f32[49152]{0:T(1024)S(1)} %div.42, f32[4]{0:T(128)S(1)} %get-tuple-element.42), kind=kOutput, calls=%fused_computation.2 | convolution fusion | flops 302579712 | bytes 26150928 | tf_op jit(solution)/shard_map/dot_general | solution.py:86
  (96 shorter events, 17.3 us)
Async XLA Ops:
  8.0 1.4 copy-start.17
  8.0 315.2 %all-reduce.2.cloned.1.call-start = ((), (), s32[]{:S(2)}) async-start(), calls=%async_computation | async-start | bytes 131072 | tf_op jit(solution)/shard_map/psum | solution.py:76
  12.7 14.6 %collective-permute-start = (f32[4,3,128,1]{2,0,3,1:T(4,128)}, f32[4,3,128,1]{2,0,3,1:T(4,128)}, u32[]{:S(2)}, u32[]{:S(2)}) collective-permute-start(f32[4,3,128,1]{2,0,3,1:T(4,128)} %copy.56), channel_id=1, source_target_pairs={{0,1},{1,2},{2,3},{3,0},{4,5},{5,6},{6,7},{7,4},{8,9},{9,10},{10,1... | collective-permute-start | bytes 18440 | tf_op jit(solution)/shard_map/ppermute | solution.py:18
  16.0 10.2 %copy-start.14 = (f32[2,2,128,384]{3,2,1,0:T(8,128)S(1)}, f32[2,2,128,384]{3,2,1,0:T(8,128)}, u32[]{:S(2)}) copy-start(f32[2,2,128,384]{3,2,1,0:T(8,128)} %param.9) | copy-start | bytes 2359300
  16.0 12.3 %collective-permute-start.1 = (f32[4,3,128,1]{2,0,3,1:T(4,128)}, f32[4,3,128,1]{2,0,3,1:T(4,128)}, u32[]{:S(2)}, u32[]{:S(2)}) collective-permute-start(f32[4,3,128,1]{2,0,3,1:T(4,128)} %copy.58), channel_id=1, source_target_pairs={{1,0},{2,1},{3,2},{0,3},{5,4},{6,5},{7,6},{4,7},{9,8},{10,9},{11,1... | collective-permute-start | bytes 18440 | tf_op jit(solution)/shard_map/ppermute | solution.py:20
  18.8 8.5 %copy-start.18 = (s32[768]{0:T(1024)S(1)}, s32[768]{0:T(1024)}, u32[]{:S(2)}) copy-start(s32[768]{0:T(1024)} %param.10) | copy-start | bytes 9220
  19.4 13.2 %collective-permute-start.2 = (f32[4,3,1,384]{3,0,2,1:T(4,128)}, f32[4,3,1,384]{3,0,2,1:T(4,128)}, u32[]{:S(2)}, u32[]{:S(2)}) collective-permute-start(f32[4,3,1,384]{3,0,2,1:T(4,128)} %copy.60), channel_id=1, source_target_pairs={{0,4},{1,5},{2,6},{3,7},{8,12},{9,13},{10,14},{11,15},{16,20},{17,... | collective-permute-start | bytes 55304 | tf_op jit(solution)/shard_map/ppermute | solution.py:18
  21.3 12.0 %collective-permute-start.3 = (f32[4,3,1,384]{3,0,2,1:T(4,128)}, f32[4,3,1,384]{3,0,2,1:T(4,128)}, u32[]{:S(2)}, u32[]{:S(2)}) collective-permute-start(f32[4,3,1,384]{3,0,2,1:T(4,128)} %copy.62), channel_id=1, source_target_pairs={{4,0},{5,1},{6,2},{7,3},{12,8},{13,9},{14,10},{15,11},{20,16},{21,... | collective-permute-start | bytes 55304 | tf_op jit(solution)/shard_map/ppermute | solution.py:20
  30.2 3.9 copy-start.8
  34.7 1.1 copy-start.2
  34.7 1.4 copy-start.4
  34.7 1.6 copy-start.6
  34.7 1.6 copy-start.10
  34.7 1.7 copy-start.12
  34.7 2.1 copy-start.13
  39.8 15.8 %collective-permute-start.4 = (f32[4,2,128,1]{3,2,0,1:T(8,128)}, f32[4,2,128,1]{3,2,0,1:T(8,128)}, u32[]{:S(2)}, u32[]{:S(2)}) collective-permute-start(f32[4,2,128,1]{3,2,0,1:T(8,128)} %get-tuple-element.36), channel_id=1, source_target_pairs={{0,1},{1,2},{2,3},{3,0},{4,5},{5,6},{6,7},{7,4},{8,9},{9,10},{10,1... | collective-permute-start | bytes 12296 | tf_op jit(solution)/shard_map/ppermute | solution.py:18
  39.9 24.5 %collective-permute-start.5 = (f32[4,2,128,1]{3,2,0,1:T(8,128)}, f32[4,2,128,1]{3,2,0,1:T(8,128)}, u32[]{:S(2)}, u32[]{:S(2)}) collective-permute-start(f32[4,2,128,1]{3,2,0,1:T(8,128)} %get-tuple-element.37), channel_id=1, source_target_pairs={{1,0},{2,1},{3,2},{0,3},{5,4},{6,5},{7,6},{4,7},{9,8},{10,9},{11,1... | collective-permute-start | bytes 12296 | tf_op jit(solution)/shard_map/ppermute | solution.py:20
  43.7 8.8 %collective-permute-start.6 = (f32[4,2,1,384]{3,0,2,1:T(4,128)}, f32[4,2,1,384]{3,0,2,1:T(4,128)}, u32[]{:S(2)}, u32[]{:S(2)}) collective-permute-start(f32[4,2,1,384]{3,0,2,1:T(4,128)} %copy.64), channel_id=1, source_target_pairs={{0,4},{1,5},{2,6},{3,7},{8,12},{9,13},{10,14},{11,15},{16,20},{17,... | collective-permute-start | bytes 36872 | tf_op jit(solution)/shard_map/ppermute | solution.py:18
  45.6 7.6 %collective-permute-start.7 = (f32[4,2,1,384]{3,0,2,1:T(4,128)}, f32[4,2,1,384]{3,0,2,1:T(4,128)}, u32[]{:S(2)}, u32[]{:S(2)}) collective-permute-start(f32[4,2,1,384]{3,0,2,1:T(4,128)} %copy.66), channel_id=1, source_target_pairs={{4,0},{5,1},{6,2},{7,3},{12,8},{13,9},{14,10},{15,11},{20,16},{21,... | collective-permute-start | bytes 36872 | tf_op jit(solution)/shard_map/ppermute | solution.py:20
  51.2 13.2 %copy-start.1 = (f32[4,128,384]{2,1,0:T(8,128)S(1)}, f32[4,128,384]{2,1,0:T(8,128)}, u32[]{:S(2)}) copy-start(f32[4,128,384]{2,1,0:T(8,128)} %copy-done) | copy-start | bytes 2359300
  51.2 13.2 %copy-start.3 = (f32[4,128,384]{2,1,0:T(8,128)S(1)}, f32[4,128,384]{2,1,0:T(8,128)}, u32[]{:S(2)}) copy-start(f32[4,128,384]{2,1,0:T(8,128)} %copy-done.2) | copy-start | bytes 2359300
  54.0 13.4 %copy-start.5 = (f32[4,128,384]{2,1,0:T(8,128)S(1)}, f32[4,128,384]{2,1,0:T(8,128)}, u32[]{:S(2)}) copy-start(f32[4,128,384]{2,1,0:T(8,128)} %copy-done.4) | copy-start | bytes 2359300
  54.0 13.4 %copy-start.7 = (f32[4,128,384]{2,1,0:T(8,128)S(1)}, f32[4,128,384]{2,1,0:T(8,128)}, u32[]{:S(2)}) copy-start(f32[4,128,384]{2,1,0:T(8,128)} %copy-done.6) | copy-start | bytes 2359300
  54.0 13.4 %copy-start.11 = (f32[4,2,128,384]{3,2,0,1:T(8,128)S(1)}, f32[4,2,128,384]{3,2,0,1:T(8,128)}, u32[]{:S(2)}) copy-start(f32[4,2,128,384]{3,2,0,1:T(8,128)} %rev.7) | copy-start | bytes 4718596
  54.0 13.4 %copy-start.15 = (f32[1,128,384]{2,1,0:T(8,128)S(1)}, f32[1,128,384]{2,1,0:T(8,128)}, u32[]{:S(2)}) copy-start(f32[1,128,384]{2,1,0:T(8,128)} %slice.146) | copy-start | bytes 589828
  54.0 13.4 %copy-start.16 = (f32[1,128,384]{2,1,0:T(8,128)S(1)}, f32[1,128,384]{2,1,0:T(8,128)}, u32[]{:S(2)}) copy-start(f32[1,128,384]{2,1,0:T(8,128)} %slice.148) | copy-start | bytes 589828
  80.9 115.0 %copy-start.20 = (f32[768]{0:T(1024)S(1)}, f32[768]{0:T(1024)}, u32[]{:S(2)}) copy-start(f32[768]{0:T(1024)} %param.12) | copy-start | bytes 9220
  195.8 1.9 copy-start.21
  195.8 1.9 copy-start.22
  197.1 348.5 %all-gather.3.cloned.1.call-start = ((), (), s32[]{:S(2)}) async-start(), calls=%async_computation.1 | async-start | bytes 25952256 | tf_op jit(solution)/shard_map/all_gather | solution.py:83
  197.7 374.6 %copy-start.19 = (f32[768,4]{0,1:T(4,128)}, f32[768,4]{0,1:T(4,128)S(1)}, u32[]{:S(2)}) copy-start(f32[768,4]{0,1:T(4,128)S(1)} %broadcast_select_fusion) | copy-start | bytes 36868
  581.6 15.3 %copy-start.9 = (f32[4,128,384]{2,1,0:T(8,128)S(1)}, f32[4,128,384]{2,1,0:T(8,128)}, u32[]{:S(2)}) copy-start(f32[4,128,384]{2,1,0:T(8,128)} %param.7) | copy-start | bytes 2359300
  (1 other events, 0.9 us)
Sparse Core Ops, SparseCore 0:
  197.2 126.0 all-reduce.1
Sparse Core Ops, SparseCore 1:
  201.5 344.0 all-gather.2
where the time goes:
time: 606 us; the launch traced here: 605 us
  waiting for transfers between devices  304 us (50%)
  blocking collectives  134 us (22%)
  local copies, waits for them, and re-layouts  66.5 us (11%)
  other arithmetic  47.3 us (8%)
  starting transfers between devices  20.3 us (3%)
  matrix products  17.3 us (3%)
  between operations  16 us (3%)
    all_gather x1, waiting for transfers between devices, on_device(): piece = lax.all_gather(theta, 'member', axis=0, tiled=True)  197 us
    all_gather x1, blocking collectives, on_device(): all_pred = lax.all_gather(own_pred, 'member', axis=1, tiled=True)  105 us
    psum x1, waiting for transfers between devices, on_device(): gram, rhs_local = lax.psum((gram_part, rhs_local), ('lat', 'lon'))  95.7 us
    psum x1, blocking collectives, on_device(): gram, rhs_local = lax.psum((gram_part, rhs_local), ('lat', 'lon'))  29.4 us
    unnamed x48, local copies, waits for them, and re-layouts  28.7 us
    dot_general x1, matrix products, on_device(): acc = jnp.dot(w_local.T, flat_piece, precision=lax.Precision.HIGHEST)  15.2 us
    ppermute x4, starting transfers between devices, padded(): lax.ppermute(head, axis, [((i + 1) % count, i) for i in range(ends)])  15.1 us
    another operation x1, local copies, waits for them, and re-layouts, on_device(): own_pred = jnp.take(c[:, 0].reshape(mem_local, -1), obs_index, axis=1).T  12.8 us
  transfers between devices with their start and end apart: 10, of which 4 were waited for; matrix products, arithmetic and copies ran while one was open for 7% of the time, Pallas kernels for 0%

commit v1 on v0

v1 whole, which is shorter than its diff:
```python
import functools

import jax
import jax.numpy as jnp
from jax import lax
from jax.experimental import pallas as pl
from jax.experimental.pallas import tpu as pltpu
from jax.sharding import PartitionSpec as P

LM = 1.0
MESH = pl.DeviceIdType.MESH
F32 = jnp.float32
BF16 = jnp.bfloat16
LANE = 128
SUB = 8


def lane_shift(x, by):
    return pltpu.roll(x, by % x.shape[1], axis=1)


def south_of(prev, cur):
    return jnp.concatenate([prev[SUB - 1 :], cur[: SUB - 1]], axis=0)


def north_of(cur, nxt):
    return jnp.concatenate([cur[1:], nxt[:1]], axis=0)


def spd_inverse(a):
    n = a.shape[0]
    row_id = lax.broadcasted_iota(jnp.int32, (n, n), 0)
    lane_id = lax.broadcasted_iota(jnp.int32, (n, n), 1)
    lane_row = lax.broadcasted_iota(jnp.int32, (1, n), 1)

    def block(_, m):
        for c in range(0, SUB, 2):
            col0 = m[:, c : c + 1]
            col1 = m[:, c + 1 : c + 2]
            row0 = m[c : c + 1, :]
            row1 = m[c + 1 : c + 2, :]
            p00 = m[c : c + 1, c : c + 1]
            p01 = m[c : c + 1, c + 1 : c + 2]
            p11 = m[c + 1 : c + 2, c + 1 : c + 2]
            inv = 1.0 / (p00 * p11 - p01 * p01)
            i00 = p11 * inv
            i01 = -p01 * inv
            i11 = p00 * inv
            row0 = jnp.where(lane_row == c, 1.0, jnp.where(lane_row == c + 1, 0.0, row0))
            row1 = jnp.where(lane_row == c, 0.0, jnp.where(lane_row == c + 1, 1.0, row1))
            new0 = i00 * row0 + i01 * row1
            new1 = i01 * row0 + i11 * row1
            pivot_lanes = (lane_id == c) | (lane_id == c + 1)
            rest = jnp.where(pivot_lanes, 0.0, m) - col0 * new0 - col1 * new1
            m = jnp.where(row_id == c, new0, jnp.where(row_id == c + 1, new1, rest))
        m = jnp.concatenate([m[SUB:], m[:SUB]], axis=0)
        return lane_shift(m, -SUB)

    return lax.fori_loop(0, n // SUB, block, a)


def kernel(
    sizes,
    theta_hbm, tracer_hbm, velocity_hbm, obs_index, obs_cell, vecs, perturb,
    out_hbm, pred_out,
    th_own, x, lat_in, east_out, west_out, east_in, west_in,
    base, diffs, faces, c1, cells,
    th_all, e_all, pred_all, pred_mat, weighted, left, g_own, rs_in, ab, upd,
    in_sem, halo_send, halo_recv, th_send, th_recv, e_send, e_recv, p_send, p_recv,
    r_send, r_recv, a_send, a_recv, o_send, o_recv,
):
    n_mem, n_lat, n_lon = sizes
    half = n_mem // 2
    tiles = n_lat * n_lon
    blocks, mem_local, rows, _ = th_own.shape
    planes, pad_rows, pad_cols = x.shape
    cols = blocks * LANE
    members = n_mem * mem_local
    half_members = members // 2
    chunk_rows = rows // half
    n_chunks = pad_rows // SUB
    obs = perturb.shape[1]
    obs_half = obs // 2
    g_rows = g_own.shape[0]
    part = g_rows // tiles
    scale = 1.0 / float(members - 1) ** 0.5

    m = lax.axis_index("member")
    la = lax.axis_index("lat")
    lo = lax.axis_index("lon")
    zh = m // half
    p = m % half
    t = la * n_lon + lo

    def at_member(peer):
        return {"member": peer, "lat": la, "lon": lo}

    def at_tile(peer):
        return {"member": m, "lat": peer // n_lon, "lon": peer % n_lon}

    loads = [
        pltpu.make_async_copy(theta_hbm.at[:, :, pl.ds(b * LANE, LANE)], th_own.at[b], in_sem.at[4 + b])
        for b in range(blocks)
    ] + [
        pltpu.make_async_copy(
            tracer_hbm, x.at[pl.ds(mem_local, 2), pl.ds(SUB, rows), pl.ds(0, cols)], in_sem.at[1]
        ),
        pltpu.make_async_copy(
            velocity_hbm, x.at[pl.ds(mem_local + 2, 4), pl.ds(SUB, rows), pl.ds(0, cols)], in_sem.at[2]
        ),
    ]
    for load in loads:
        load.start()

    barrier = pltpu.get_barrier_semaphore()

    def greet_member(d, _):
        pl.semaphore_signal(barrier, inc=1, device_id=at_member((m + d) % n_mem), device_id_type=MESH)
        return 0

    def greet_tile(d, _):
        pl.semaphore_signal(barrier, inc=1, device_id=at_tile((t + d) % tiles), device_id_type=MESH)
        return 0

    lax.fori_loop(1, n_mem, greet_member, 0)
    lax.fori_loop(1, tiles, greet_tile, 0)

    def row_of(i):
        return jnp.concatenate([vecs[i, b : b + 1, :] for b in range(obs // LANE)], axis=1)

    observed = row_of(0)
    noise = row_of(1)
    inv_noise = 1.0 / noise
    e_own = observed + jnp.sqrt(noise) * perturb[...]
    e_all[p, 0:mem_local, :] = e_own[:, :obs_half]
    e_all[p, mem_local:SUB, :] = e_own[:, obs_half:]

    for load in loads[:blocks]:
        load.wait()

    def make_kappa(i, _):
        r = pl.multiple_of(i * SUB, SUB)
        for j in range(mem_local):
            for b in range(blocks):
                x[j, pl.ds(r + SUB, SUB), pl.ds(b * LANE, LANE)] = 0.1 * jax.nn.sigmoid(
                    th_own[b, j, pl.ds(r, SUB), :]
                )
        return 0

    lax.fori_loop(0, rows // SUB, make_kappa, 0)
    for load in loads[blocks:]:
        load.wait()

    lane8 = lax.broadcasted_iota(jnp.int32, (SUB, LANE), 1)
    sub8 = lax.broadcasted_iota(jnp.int32, (SUB, LANE), 0)

    def pack(i, _):
        r = pl.multiple_of(i * SUB, SUB)
        east = jnp.zeros((SUB, LANE), F32)
        west = jnp.zeros((SUB, LANE), F32)
        for q in range(planes):
            first = x[q, pl.ds(r + SUB, SUB), pl.ds(0, LANE)]
            last = x[q, pl.ds(r + SUB, SUB), pl.ds(cols - LANE, LANE)]
            east = jnp.where((lane8 // 2) == q, lane_shift(first, 2 * q), east)
            west = jnp.where(((LANE - 1 - lane8) // 2) == q, lane_shift(last, -2 * q), west)
        east_out[pl.ds(r, SUB), :] = east
        west_out[pl.ds(r, SUB), :] = west
        return 0

    lax.fori_loop(0, rows // SUB, pack, 0)

    pl.semaphore_wait(barrier, n_mem - 1 + tiles - 1)

    my_edge = pl.multiple_of((1 - la) * (rows - SUB), SUB)
    their_edge = pl.multiple_of(la * (rows + SUB), SUB)
    lo_w = (lo + n_lon - 1) % n_lon
    lo_e = (lo + 1) % n_lon

    def halo(i, src, dst, lat, lon):
        return pltpu.make_async_remote_copy(
            src_ref=src, dst_ref=dst, send_sem=halo_send.at[i], recv_sem=halo_recv.at[i],
            device_id={"member": m, "lat": lat, "lon": lon}, device_id_type=MESH,
        )

    halos = [
        halo(0, east_out, east_in.at[pl.ds(SUB, rows), :], la, lo_w),
        halo(1, west_out, west_in.at[pl.ds(SUB, rows), :], la, lo_e),
        halo(2, east_out.at[pl.ds(my_edge, SUB), :], east_in.at[pl.ds(their_edge, SUB), :], 1 - la, lo_w),
        halo(3, west_out.at[pl.ds(my_edge, SUB), :], west_in.at[pl.ds(their_edge, SUB), :], 1 - la, lo_e),
        halo(4, x.at[:, pl.ds(my_edge + SUB, SUB), pl.ds(0, cols)], lat_in, 1 - la, lo),
    ]
    for copy in halos:
        copy.start()

    def e_copy(d):
        peer = (p + d) % half
        return pltpu.make_async_remote_copy(
            src_ref=e_all.at[p], dst_ref=e_all.at[p], send_sem=e_send.at[peer], recv_sem=e_recv.at[p],
            device_id=at_member(zh * half + peer), device_id_type=MESH,
        )

    def e_arrival(d):
        peer = (p + d) % half
        return pltpu.make_async_remote_copy(
            src_ref=e_all.at[p], dst_ref=e_all.at[peer], send_sem=e_send.at[peer], recv_sem=e_recv.at[peer],
            device_id=at_member(zh * half + peer), device_id_type=MESH,
        )

    def th_copy(d):
        peer = (m + d) % n_mem
        r = pl.multiple_of((peer % half) * chunk_rows, chunk_rows)
        return pltpu.make_async_remote_copy(
            src_ref=th_own.at[:, :, pl.ds(r, chunk_rows), :],
            dst_ref=th_all.at[:, pl.ds(m * mem_local, mem_local)],
            send_sem=th_send.at[peer], recv_sem=th_recv.at[m],
            device_id=at_member(peer), device_id_type=MESH,
        )

    def th_arrival(d):
        peer = (m + d) % n_mem
        return pltpu.make_async_remote_copy(
            src_ref=th_own.at[:, :, pl.ds(0, chunk_rows), :],
            dst_ref=th_all.at[:, pl.ds(peer * mem_local, mem_local)],
            send_sem=th_send.at[peer], recv_sem=th_recv.at[peer],
            device_id=at_member(peer), device_id_type=MESH,
        )

    def start(copy):
        def body(d, _):
            copy(d).start()
            return 0
        return body

    def wait_recv(copy):
        def body(d, _):
            copy(d).wait_recv()
            return 0
        return body

    def wait_send(copy):
        def body(d, _):
            copy(d).wait_send()
            return 0
        return body

    lax.fori_loop(1, half, start(e_copy), 0)
    lax.fori_loop(1, n_mem, start(th_copy), 0)
    own_chunk = pl.multiple_of(p * chunk_rows, chunk_rows)
    own_th = pltpu.make_async_copy(
        th_own.at[:, :, pl.ds(own_chunk, chunk_rows), :],
        th_all.at[:, pl.ds(m * mem_local, mem_local)],
        in_sem.at[3],
    )
    own_th.start()

    for copy in halos:
        copy.wait_recv()

    for q in range(planes):
        block = lat_in[q]
        x[q, 0:SUB, 0:cols] = jnp.where(la == 1, block, 0.0)
        x[q, pad_rows - SUB : pad_rows, 0:cols] = jnp.where(la == 0, block, 0.0)

    def unpack(i, _):
        r = pl.multiple_of(i * SUB, SUB)
        inside = ((i > 0) | (la == 1)) & ((i < n_chunks - 1) | (la == 0))
        east = jnp.where(inside, east_in[pl.ds(r, SUB), :], 0.0)
        west = jnp.where(inside, west_in[pl.ds(r, SUB), :], 0.0)
        for q in range(planes):
            x[q, pl.ds(r, SUB), pl.ds(cols, LANE)] = jnp.where(
                lane8 < LANE // 2, lane_shift(east, -2 * q), lane_shift(west, 2 * q)
            )
        return 0

    lax.fori_loop(0, n_chunks, unpack, 0)

    def shared(i, _):
        r = pl.multiple_of(i * SUB, SUB)
        before = pl.multiple_of(jnp.maximum(i - 1, 0) * SUB, SUB)
        after = pl.multiple_of(jnp.minimum(i + 1, n_chunks - 1) * SUB, SUB)
        cur = [x[mem_local + l, pl.ds(r, SUB), :] for l in range(2)]
        for l in range(2):
            c = cur[l]
            u = x[mem_local + 2 + l, pl.ds(r, SUB), :]
            v = x[mem_local + 4 + l, pl.ds(r, SUB), :]
            d_w = lane_shift(c, 1) - c
            d_e = lane_shift(c, -1) - c
            d_s = south_of(x[mem_local + l, pl.ds(before, SUB), :], c) - c
            d_n = north_of(c, x[mem_local + l, pl.ds(after, SUB), :]) - c
            adv = jnp.maximum(u, 0.0) * d_w - jnp.minimum(u, 0.0) * d_e
            adv = adv + jnp.maximum(v, 0.0) * d_s - jnp.minimum(v, 0.0) * d_n
            base[l, pl.ds(r, SUB), :] = c + adv + 0.2 * (cur[1 - l] - c)
            for k, d in enumerate((d_w, d_e, d_s, d_n)):
                diffs[l, k, pl.ds(r, SUB), :] = d
        return 0

    lax.fori_loop(0, n_chunks, shared, 0)

    def first_step(i, _):
        r = pl.multiple_of(i * SUB, SUB)
        before = pl.multiple_of(jnp.maximum(i - 1, 0) * SUB, SUB)
        after = pl.multiple_of(jnp.minimum(i + 1, n_chunks - 1) * SUB, SUB)
        inside = ((i > 0) | (la == 1)) & ((i < n_chunks - 1) | (la == 0))
        for j in range(mem_local):
            k = x[j, pl.ds(r, SUB), :]
            f_e = 0.5 * (k + lane_shift(k, -1))
            f_w = lane_shift(f_e, 1)
            f_s = 0.5 * (k + south_of(x[j, pl.ds(before, SUB), :], k))
            f_n = 0.5 * (k + north_of(k, x[j, pl.ds(after, SUB), :]))
            for n, f in enumerate((f_w, f_e, f_s, f_n)):
                faces[j, n, pl.ds(r, SUB), :] = f
            for l in range(2):
                c = base[l, pl.ds(r, SUB), :]
                for n, f in enumerate((f_w, f_e, f_s, f_n)):
                    c = c + f * diffs[l, n, pl.ds(r, SUB), :]
                c1[j, l, pl.ds(r, SUB), :] = jnp.where(inside, c, 0.0)
        return 0

    lax.fori_loop(0, n_chunks, first_step, 0)

    flat_cells = cells.reshape(rows * blocks * SUB, LANE)

    def second_step(i, _):
        r = pl.multiple_of(i * SUB, SUB)
        before = pl.multiple_of((i - 1) * SUB, SUB)
        after = pl.multiple_of((i + 1) * SUB, SUB)
        u = x[mem_local + 2, pl.ds(r, SUB), pl.ds(0, cols)]
        v = x[mem_local + 4, pl.ds(r, SUB), pl.ds(0, cols)]
        winds = (jnp.maximum(u, 0.0), -jnp.minimum(u, 0.0), jnp.maximum(v, 0.0), -jnp.minimum(v, 0.0))
        for j in range(mem_local):
            wide = c1[j, 0, pl.ds(r, SUB), :]
            c = wide[:, :cols]
            sides = (
                lane_shift(wide, 1)[:, :cols],
                lane_shift(wide, -1)[:, :cols],
                south_of(c1[j, 0, pl.ds(before, SUB), pl.ds(0, cols)], c),
                north_of(c, c1[j, 0, pl.ds(after, SUB), pl.ds(0, cols)]),
            )
            new = c + 0.2 * (c1[j, 1, pl.ds(r, SUB), pl.ds(0, cols)] - c)
            for n in range(4):
                new = new + (winds[n] + faces[j, n, pl.ds(r, SUB), pl.ds(0, cols)]) * (sides[n] - c)
            for b in range(blocks):
                first = ((i - 1) * SUB * blocks + b) * SUB + j
                piece = new[:, b * LANE : (b + 1) * LANE]
                flat_cells[pl.ds(first, SUB, stride=SUB * blocks), :] = piece
                flat_cells[pl.ds(first + mem_local, SUB, stride=SUB * blocks), :] = piece
        return 0

    lax.fori_loop(1, n_chunks - 1, second_step, 0)

    obs_blocks = obs // LANE
    step_of = 8
    obs_lane = [
        jnp.broadcast_to(obs_cell[b : b + 1, :] & (LANE - 1), (SUB, LANE)) for b in range(obs_blocks)
    ]

    def gather(i, accs):
        accs = list(accs)
        for k in range(step_of):
            s = i * step_of + k
            for b in range(obs_blocks):
                block = lax.shift_right_logical(obs_index[b * LANE + s], LANE.bit_length() - 1)
                got = cells[block]
                got = jnp.take_along_axis(got, obs_lane[b], axis=1, mode="promise_in_bounds")
                h = b // (obs_blocks // 2)
                here = (lane8 == s) & (sub8 // mem_local == h)
                a = b % (obs_blocks // 2)
                accs[a] = jnp.where(here, got, accs[a])
        return tuple(accs)

    accs = lax.fori_loop(
        0, LANE // step_of, gather, tuple(jnp.zeros((SUB, LANE), F32) for _ in range(obs_blocks // 2))
    )
    own_pred = jnp.concatenate(accs, axis=1)
    pred_all[m] = own_pred
    pred_out[:, 0:obs_half] = own_pred[0:mem_local]
    pred_out[:, obs_half:obs] = own_pred[mem_local:SUB]

    def p_copy(d):
        peer = (m + d) % n_mem
        return pltpu.make_async_remote_copy(
            src_ref=pred_all.at[m], dst_ref=pred_all.at[m], send_sem=p_send.at[peer], recv_sem=p_recv.at[m],
            device_id=at_member(peer), device_id_type=MESH,
        )

    def p_arrival(d):
        peer = (m + d) % n_mem
        return pltpu.make_async_remote_copy(
            src_ref=pred_all.at[m], dst_ref=pred_all.at[peer], send_sem=p_send.at[peer], recv_sem=p_recv.at[peer],
            device_id=at_member(peer), device_id_type=MESH,
        )

    lax.fori_loop(1, n_mem, start(p_copy), 0)
    lax.fori_loop(1, half, wait_recv(e_arrival), 0)
    lax.fori_loop(1, n_mem, wait_recv(p_arrival), 0)

    low = lax.broadcasted_iota(jnp.int32, (SUB, obs_half), 0) < mem_local

    def unfold(a, b):
        top = jnp.where(low, a, pltpu.roll(b, mem_local, axis=0))
        bottom = jnp.where(low, pltpu.roll(a, mem_local, axis=0), b)
        return jnp.concatenate([top, bottom], axis=1)

    def collect(i, total):
        both = unfold(pred_all[2 * i], pred_all[2 * i + 1])
        pred_mat[pl.ds(pl.multiple_of(i * SUB, SUB), SUB), :] = both
        return total + both

    total = lax.fori_loop(0, n_mem // 2, collect, jnp.zeros((SUB, obs), F32))
    mean = jnp.sum(total, axis=0, keepdims=True) * (1.0 / members)

    def center(i, _):
        r = pl.multiple_of(i * SUB, SUB)
        anom = (pred_mat[pl.ds(r, SUB), :] - mean) * scale
        left[pl.ds(r, SUB), :] = anom
        weighted[pl.ds(r, SUB), :] = anom * inv_noise
        return 0

    lax.fori_loop(0, members // SUB, center, 0)

    def innovate(i, _):
        r = pl.multiple_of(zh * half_members + i * SUB, SUB)
        e = unfold(e_all[2 * i], e_all[2 * i + 1])
        left[pl.ds(pl.multiple_of(members + i * SUB, SUB), SUB), :] = e - pred_mat[pl.ds(r, SUB), :]
        return 0

    lax.fori_loop(0, half_members // SUB, innovate, 0)

    g_own[...] = lax.dot_general(
        left[...], weighted[...], (((1,), (1,)), ((), ())), precision=lax.Precision.HIGHEST,
        preferred_element_type=F32,
    )

    def r_copy(d):
        peer = (t + d) % tiles
        return pltpu.make_async_remote_copy(
            src_ref=g_own.at[pl.ds(pl.multiple_of(peer * part, SUB), part), :], dst_ref=rs_in.at[t],
            send_sem=r_send.at[peer], recv_sem=r_recv.at[t],
            device_id=at_tile(peer), device_id_type=MESH,
        )

    def r_arrival(d):
        peer = (t + d) % tiles
        return pltpu.make_async_remote_copy(
            src_ref=g_own.at[pl.ds(0, part), :], dst_ref=rs_in.at[peer],
            send_sem=r_send.at[peer], recv_sem=r_recv.at[peer],
            device_id=at_tile(peer), device_id_type=MESH,
        )

    my_part = pl.multiple_of(t * part, SUB)
    lax.fori_loop(1, tiles, start(r_copy), 0)
    rs_in[t] = g_own[pl.ds(my_part, part), :]
    lax.fori_loop(1, tiles, wait_recv(r_arrival), 0)
    total_part = rs_in[0]
    for k in range(1, tiles):
        total_part = total_part + rs_in[k]
    ab[pl.ds(my_part, part), :] = total_part

    def a_copy(d):
        peer = (t + d) % tiles
        mine = ab.at[pl.ds(my_part, part), :]
        return pltpu.make_async_remote_copy(
            src_ref=mine, dst_ref=mine, send_sem=a_send.at[peer], recv_sem=a_recv.at[t],
            device_id=at_tile(peer), device_id_type=MESH,
        )

    def a_arrival(d):
        peer = (t + d) % tiles
        return pltpu.make_async_remote_copy(
            src_ref=ab.at[pl.ds(my_part, part), :],
            dst_ref=ab.at[pl.ds(pl.multiple_of(peer * part, SUB), part), :],
            send_sem=a_send.at[peer], recv_sem=a_recv.at[peer],
            device_id=at_tile(peer), device_id_type=MESH,
        )

    lax.fori_loop(1, tiles, start(a_copy), 0)
    lax.fori_loop(1, tiles, wait_recv(a_arrival), 0)

    eye = lax.broadcasted_iota(jnp.int32, (members, members), 0) == lax.broadcasted_iota(
        jnp.int32, (members, members), 1
    )
    inverse = spd_inverse(ab[0:members, :] + jnp.where(eye, LM, 0.0))
    w = jnp.dot(
        ab[members : members + half_members, :], inverse, precision=lax.Precision.HIGHEST,
        preferred_element_type=F32,
    )
    w = scale * (w - jnp.mean(w, axis=1, keepdims=True))
    w_hi = w.astype(BF16)
    w_lo = (w - w_hi.astype(F32)).astype(BF16)
    lhs = jnp.concatenate(
        [jnp.concatenate([w_hi, w_hi], axis=1), jnp.concatenate([w_lo, jnp.zeros_like(w_lo)], axis=1)], axis=0
    )

    own_th.wait()
    lax.fori_loop(1, n_mem, wait_recv(th_arrival), 0)

    def o_copy(b, d):
        peer = (p + d) % half
        return pltpu.make_async_remote_copy(
            src_ref=upd.at[b, pl.ds(peer * mem_local, mem_local)],
            dst_ref=out_hbm.at[:, pl.ds(own_chunk, chunk_rows), pl.ds(b * LANE, LANE)],
            send_sem=o_send.at[b, peer], recv_sem=o_recv.at[b, p],
            device_id=at_member(zh * half + peer), device_id_type=MESH,
        )

    def o_arrival(b, d):
        peer = (p + d) % half
        return pltpu.make_async_remote_copy(
            src_ref=upd.at[b, pl.ds(peer * mem_local, mem_local)],
            dst_ref=out_hbm.at[
                :, pl.ds(pl.multiple_of(peer * chunk_rows, chunk_rows), chunk_rows), pl.ds(b * LANE, LANE)
            ],
            send_sem=o_send.at[b, peer], recv_sem=o_recv.at[b, peer],
            device_id=at_member(zh * half + peer), device_id_type=MESH,
        )

    flat = th_all.reshape(blocks * members * chunk_rows, LANE)
    upd_flat = upd.reshape(blocks * half_members * chunk_rows, LANE)
    own_out = []
    for b in range(blocks):
        at_b = b * members * chunk_rows
        for r in range(0, chunk_rows, 2):
            field = jnp.concatenate(
                [flat[pl.ds(at_b + r + k, members, stride=chunk_rows), :] for k in range(2)], axis=1
            )
            hi = field.astype(BF16)
            lo_part = (field - hi.astype(F32)).astype(BF16)
            both = jnp.dot(lhs, jnp.concatenate([hi, lo_part], axis=0), preferred_element_type=F32)
            both = both[:half_members] + both[half_members:]
            for k in range(2):
                own = flat[pl.ds(at_b + zh * (half_members * chunk_rows) + r + k, half_members, stride=chunk_rows), :]
                upd_flat[pl.ds(b * half_members * chunk_rows + r + k, half_members, stride=chunk_rows), :] = (
                    own + both[:, k * LANE : (k + 1) * LANE]
                )
        lax.fori_loop(1, half, start(functools.partial(o_copy, b)), 0)
        own_out.append(
            pltpu.make_async_copy(
                upd.at[b, pl.ds(p * mem_local, mem_local)],
                out_hbm.at[:, pl.ds(own_chunk, chunk_rows), pl.ds(b * LANE, LANE)],
                in_sem.at[4 + b],
            )
        )
        own_out[b].start()

    for copy in halos:
        copy.wait_send()
    lax.fori_loop(1, half, wait_send(e_copy), 0)
    lax.fori_loop(1, n_mem, wait_send(th_copy), 0)
    lax.fori_loop(1, n_mem, wait_send(p_copy), 0)
    lax.fori_loop(1, tiles, wait_send(r_copy), 0)
    lax.fori_loop(1, tiles, wait_send(a_copy), 0)
    for b in range(blocks):
        own_out[b].wait()
        lax.fori_loop(1, half, wait_recv(functools.partial(o_arrival, b)), 0)
        lax.fori_loop(1, half, wait_send(functools.partial(o_copy, b)), 0)


def on_device(sizes, theta, tracer, velocity, obs_index, observed, noise_var, obs_perturb):
    n_mem, n_lat, n_lon = sizes
    mem_local, rows, cols = theta.shape
    obs = obs_index.shape[0]
    half = n_mem // 2
    tiles = n_lat * n_lon
    members = n_mem * mem_local
    half_members = members // 2
    chunk_rows = rows // half
    planes = mem_local + 6
    pad_rows, pad_cols = rows + 2 * SUB, cols + LANE
    g_rows = members + half_members
    vecs = jnp.stack([observed.reshape(obs // LANE, LANE), noise_var.reshape(obs // LANE, LANE)])
    dma = pltpu.SemaphoreType.DMA
    theta_new, pred = pl.pallas_call(
        functools.partial(kernel, sizes),
        out_shape=(
            jax.ShapeDtypeStruct(theta.shape, F32),
            jax.ShapeDtypeStruct((mem_local, obs), F32),
        ),
        in_specs=[
            pl.BlockSpec(memory_space=pl.ANY),
            pl.BlockSpec(memory_space=pl.ANY),
            pl.BlockSpec(memory_space=pl.ANY),
            pl.BlockSpec(memory_space=pltpu.SMEM),
            pl.BlockSpec(memory_space=pltpu.VMEM),
            pl.BlockSpec(memory_space=pltpu.VMEM),
            pl.BlockSpec(memory_space=pltpu.VMEM),
        ],
        out_specs=(pl.BlockSpec(memory_space=pl.ANY), pl.BlockSpec(memory_space=pltpu.VMEM)),
        scratch_shapes=[
            pltpu.VMEM((cols // LANE, mem_local, rows, LANE), F32),
            pltpu.VMEM((planes, pad_rows, pad_cols), F32),
            pltpu.VMEM((planes, SUB, cols), F32),
            pltpu.VMEM((rows, LANE), F32),
            pltpu.VMEM((rows, LANE), F32),
            pltpu.VMEM((pad_rows, LANE), F32),
            pltpu.VMEM((pad_rows, LANE), F32),
            pltpu.VMEM((2, pad_rows, pad_cols), F32),
            pltpu.VMEM((2, 4, pad_rows, pad_cols), F32),
            pltpu.VMEM((mem_local, 4, pad_rows, pad_cols), F32),
            pltpu.VMEM((mem_local, 2, pad_rows, pad_cols), F32),
            pltpu.VMEM((rows * (cols // LANE), SUB, LANE), F32),
            pltpu.VMEM((cols // LANE, members, chunk_rows, LANE), F32),
            pltpu.VMEM((half, SUB, obs // 2), F32),
            pltpu.VMEM((n_mem, SUB, obs // 2), F32),
            pltpu.VMEM((members, obs), F32),
            pltpu.VMEM((members, obs), F32),
            pltpu.VMEM((g_rows, obs), F32),
            pltpu.VMEM((g_rows, members), F32),
            pltpu.VMEM((tiles, g_rows // tiles, members), F32),
            pltpu.VMEM((g_rows, members), F32),
            pltpu.VMEM((cols // LANE, half_members, chunk_rows, LANE), F32),
            dma((4 + cols // LANE,)),
            dma((5,)), dma((5,)),
            dma((n_mem,)), dma((n_mem,)),
            dma((half,)), dma((half,)),
            dma((n_mem,)), dma((n_mem,)),
            dma((tiles,)), dma((tiles,)),
            dma((tiles,)), dma((tiles,)),
            dma((cols // LANE, half)), dma((cols // LANE, half)),
        ],
        compiler_params=pltpu.CompilerParams(
            collective_id=0, has_side_effects=True, vmem_limit_bytes=56 * 1024 * 1024
        ),
        name="inversion",
    )(theta, tracer, velocity.reshape(4, rows, cols), obs_index, obs_index.reshape(obs // LANE, LANE), vecs, obs_perturb.T)
    return theta_new, pred.T


def solution(mesh):
    placed = (
        P("member", "lat", "lon"),
        P(None, "lat", "lon"),
        P(None, None, "lat", "lon"),
        P(("lat", "lon")),
        P(("lat", "lon")),
        P(("lat", "lon")),
        P(("lat", "lon"), "member"),
    )
    sizes = (mesh.shape["member"], mesh.shape["lat"], mesh.shape["lon"])
    return jax.shard_map(
        functools.partial(on_device, sizes),
        mesh=mesh,
        in_specs=placed,
        out_specs=(P("member", "lat", "lon"), P(("lat", "lon"), "member")),
        check_vma=False,
    )
```

time: 606 us -> 108 us (0.18)
  waiting for transfers between devices: 304 us -> 0 us
  blocking collectives: 134 us -> 0 us
  Pallas kernels: 0 us -> 103 us
  local copies, waits for them, and re-layouts: 66.5 us -> 3.36 us
  other arithmetic: 47.3 us -> 0.6 us
  starting transfers between devices: 20.3 us -> 0 us
  matrix products: 17.3 us -> 0 us
  between operations: 16 us -> 0.66 us
    all_gather x1 -> x0, waiting for transfers between devices: 197 us -> none  [on_device(): piece = lax.all_gather(theta, 'member', axis=0, tiled=True)]
    all_gather x1 -> x0, blocking collectives: 105 us -> none  [on_device(): all_pred = lax.all_gather(own_pred, 'member', axis=1, tiled=True)]
    pallas_call x0 -> x1, Pallas kernels: none -> 103 us  [on_device(): pl.pallas_call(functools.partial(kernel, sizes), out_shape=(jax.ShapeDtyp...]
    psum x1 -> x0, waiting for transfers between devices: 95.7 us -> none  [on_device(): gram, rhs_local = lax.psum((gram_part, rhs_local), ('lat', 'lon'))]
    psum x1 -> x0, blocking collectives: 29.4 us -> none  [on_device(): gram, rhs_local = lax.psum((gram_part, rhs_local), ('lat', 'lon'))]
    unnamed x48 -> x8, local copies, waits for them, and re-layouts: 28.7 us -> 3.36 us
    another operation x5 -> x1, other arithmetic: 22.9 us -> 0.6 us  [on_device(): jnp.stack([observed.reshape(obs // LANE, LANE), noise_var.reshape(obs //...]
    ppermute x8 -> x0, starting transfers between devices: 20.2 us -> none  [the longest x4 15.1 us: padded(): lax.ppermute(head, axis, [((i + 1) % count, i) for i in range(ends)])]
  transfers between devices with their start and end apart: 10 -> 0, of which waited for: 4 -> 0; matrix products, arithmetic and copies ran while one was open for 7% -> 0% of each run, Pallas kernels for 0% -> 0%
where the time goes in v1:
time: 108 us; the launch traced here: 107 us
  Pallas kernels  103 us (95%)
  local copies, waits for them, and re-layouts  3.36 us (3%)
    pallas_call x1, Pallas kernels, on_device(): pl.pallas_call(functools.partial(kernel, sizes), out_shape=(jax.ShapeDtyp...  103 us
    unnamed x8, local copies, waits for them, and re-layouts  3.36 us

profile of v1, /device:TPU:1, one launch (start us, length us, event | category | flops | bytes accessed | tf_op | source)
XLA Modules:
  0.0 107.3 jit_solution(17647146360239943622)
XLA Ops:
  0.6 0.0 copy-start.2
  0.6 0.0 copy-start.1
  0.6 0.7 copy-done.2
  1.3 0.0 copy-done.1
  1.3 0.6 pad_maximum_fusion.vecs
  1.9 102.6 %inversion.1 = (f32[4,128,384]{2,1,0:T(8,128)}, f32[4,768]{1,0:T(4,128)}) custom-call(f32[4,128,384]{2,1,0:T(8,128)} %theta_hbm.1, f32[2,128,384]{2,1,0:T(8,128)} %tracer_hbm.1, f32[4,128,384]{2,1,0:T(8,128)} %bitcast.6, s32[768]{0:T(1024)} %obs_index.1, s32[6,128]{1,0:T(8,128)} %bitcast.7, f32[2,6,128]{2,1,0:T(8,128)} %pad_maximum_fusion.vecs, f32[4,768]{1,0:T(4,128)} %bitcast.8), custom_call_target="tpu_custom_call" | custom-call | tf_op jit(solution)/shard_map/inversion/pallas_call | solution.py:572
  104.6 0.0 copy-start
  104.6 2.1 %copy.11 = f32[4,128,384]{2,1,0:T(8,128)} copy(f32[4,128,384]{2,1,0:T(8,128)} %get-tuple-element.8) | data formatting | bytes 1572864
  106.7 0.0 copy-done
  106.7 0.6 copy.12
Async XLA Ops:
  0.6 0.7 copy-start.2
  0.6 0.7 copy-start.1
  104.6 2.1 %copy-start = (f32[4,768]{1,0:T(4,128)S(1)}, f32[4,768]{1,0:T(4,128)}, u32[]{:S(2)}) copy-start(f32[4,768]{1,0:T(4,128)} %get-tuple-element.5) | copy-start | bytes 36868

commit v2 on v1

--- a/solution.py
+++ b/solution.py
@@ -13,6 +13,7 @@
 BF16 = jnp.bfloat16
 LANE = 128
 SUB = 8
+FAR = (6, 4, 4, 4, 4, 4, 4, 4)
 
 
 def lane_shift(x, by):
@@ -27,46 +28,78 @@
     return jnp.concatenate([cur[1:], nxt[:1]], axis=0)
 
 
-def spd_inverse(a):
-    n = a.shape[0]
-    row_id = lax.broadcasted_iota(jnp.int32, (n, n), 0)
-    lane_id = lax.broadcasted_iota(jnp.int32, (n, n), 1)
-    lane_row = lax.broadcasted_iota(jnp.int32, (1, n), 1)
-
-    def block(_, m):
+def invert(mat):
+    n = mat.shape[0]
+    shape = (SUB, n)
+    row_id = lax.broadcasted_iota(jnp.int32, shape, 0)
+    lane_id = lax.broadcasted_iota(jnp.int32, shape, 1)
+
+    def row(x, r):
+        return jnp.broadcast_to(x[r : r + 1, :], shape)
+
+    def behind(first, panel):
+        lanes = [jnp.full(shape, (first + c) & (n - 1), jnp.int32) for c in range(SUB)]
+        rows = [row(panel, c) for c in range(SUB)]
+        in_panel = (lane_id >= first) & (lane_id < first + SUB)
+
+        def update(tile):
+            parts = [
+                jnp.take_along_axis(tile, lanes[c], axis=1, mode="promise_in_bounds") * rows[c] for c in range(SUB)
+            ]
+            while len(parts) > 1:
+                parts = [parts[k] + parts[k + 1] for k in range(0, len(parts), 2)]
+            return jnp.where(in_panel, 0.0, tile) - parts[0]
+
+        return update
+
+    def eliminate_panel(b, last):
+        first = pl.multiple_of(b * SUB, SUB)
+        update = behind(first - SUB, last)
+        panel = update(mat[pl.ds(first, SUB), :])
+        cols = [
+            jnp.take_along_axis(panel, jnp.full(shape, first + c, jnp.int32), axis=1, mode="promise_in_bounds")
+            for c in range(SUB)
+        ]
         for c in range(0, SUB, 2):
-            col0 = m[:, c : c + 1]
-            col1 = m[:, c + 1 : c + 2]
-            row0 = m[c : c + 1, :]
-            row1 = m[c + 1 : c + 2, :]
-            p00 = m[c : c + 1, c : c + 1]
-            p01 = m[c : c + 1, c + 1 : c + 2]
-            p11 = m[c + 1 : c + 2, c + 1 : c + 2]
+            c0, c1 = cols[c], cols[c + 1]
+            p00, p01, p11 = row(c0, c), row(c1, c), row(c1, c + 1)
             inv = 1.0 / (p00 * p11 - p01 * p01)
-            i00 = p11 * inv
-            i01 = -p01 * inv
-            i11 = p00 * inv
-            row0 = jnp.where(lane_row == c, 1.0, jnp.where(lane_row == c + 1, 0.0, row0))
-            row1 = jnp.where(lane_row == c, 0.0, jnp.where(lane_row == c + 1, 1.0, row1))
-            new0 = i00 * row0 + i01 * row1
-            new1 = i01 * row0 + i11 * row1
-            pivot_lanes = (lane_id == c) | (lane_id == c + 1)
-            rest = jnp.where(pivot_lanes, 0.0, m) - col0 * new0 - col1 * new1
-            m = jnp.where(row_id == c, new0, jnp.where(row_id == c + 1, new1, rest))
-        m = jnp.concatenate([m[SUB:], m[:SUB]], axis=0)
-        return lane_shift(m, -SUB)
-
-    return lax.fori_loop(0, n // SUB, block, a)
+            i00, i01, i11 = p11 * inv, -p01 * inv, p00 * inv
+
+            def eliminate(r0, r1, rest):
+                new0 = i00 * r0 + i01 * r1
+                new1 = i01 * r0 + i11 * r1
+                rest = rest - c0 * new0 - c1 * new1
+                return jnp.where(row_id == c, new0, jnp.where(row_id == c + 1, new1, rest))
+
+            at0, at1 = lane_id == first + c, lane_id == first + c + 1
+            for k in range(c + 2, SUB):
+                cols[k] = eliminate(row(cols[k], c), row(cols[k], c + 1), cols[k])
+            panel = eliminate(
+                jnp.where(at0, 1.0, jnp.where(at1, 0.0, row(panel, c))),
+                jnp.where(at0, 0.0, jnp.where(at1, 1.0, row(panel, c + 1))),
+                jnp.where(at0 | at1, 0.0, panel),
+            )
+        for i in range(n // SUB):
+            tile = mat[i * SUB : (i + 1) * SUB, :]
+            mat[i * SUB : (i + 1) * SUB, :] = jnp.where(b - 1 == i, tile, update(tile))
+        mat[pl.ds(first, SUB), :] = panel
+        return panel
+
+    last = lax.fori_loop(0, n // SUB, eliminate_panel, jnp.zeros(shape, F32))
+    update = behind(n - SUB, last)
+    for i in range(n // SUB - 1):
+        mat[i * SUB : (i + 1) * SUB, :] = update(mat[i * SUB : (i + 1) * SUB, :])
 
 
 def kernel(
     sizes,
-    theta_hbm, tracer_hbm, velocity_hbm, obs_index, obs_cell, vecs, perturb,
+    theta_hbm, tracer_hbm, velocity_hbm, obs_index, obs_cell, observed_in, noise_in, perturb,
     out_hbm, pred_out,
     th_own, x, lat_in, east_out, west_out, east_in, west_in,
     base, diffs, faces, c1, cells,
-    th_all, e_all, pred_all, pred_mat, weighted, left, g_own, rs_in, ab, upd,
-    in_sem, halo_send, halo_recv, th_send, th_recv, e_send, e_recv, p_send, p_recv,
+    th_all, e_all, pred_all, pred_mat, weighted, left, g_own, rs_in, ab, mat, upd,
+    in_sem, halo_send, halo_recv, th_send, th_recv, f_send, f_recv, e_send, e_recv, p_send, p_recv,
     r_send, r_recv, a_send, a_recv, o_send, o_recv,
 ):
     n_mem, n_lat, n_lon = sizes
@@ -88,15 +121,15 @@
     m = lax.axis_index("member")
     la = lax.axis_index("lat")
     lo = lax.axis_index("lon")
-    zh = m // half
-    p = m % half
+    zh = lax.shift_right_logical(m, half.bit_length() - 1)
+    p = m & (half - 1)
     t = la * n_lon + lo
 
     def at_member(peer):
         return {"member": peer, "lat": la, "lon": lo}
 
     def at_tile(peer):
-        return {"member": m, "lat": peer // n_lon, "lon": peer % n_lon}
+        return {"member": m, "lat": lax.shift_right_logical(peer, n_lon.bit_length() - 1), "lon": peer & (n_lon - 1)}
 
     loads = [
         pltpu.make_async_copy(theta_hbm.at[:, :, pl.ds(b * LANE, LANE)], th_own.at[b], in_sem.at[4 + b])
@@ -115,21 +148,21 @@
     barrier = pltpu.get_barrier_semaphore()
 
     def greet_member(d, _):
-        pl.semaphore_signal(barrier, inc=1, device_id=at_member((m + d) % n_mem), device_id_type=MESH)
+        pl.semaphore_signal(barrier, inc=1, device_id=at_member(m ^ d), device_id_type=MESH)
         return 0
 
     def greet_tile(d, _):
-        pl.semaphore_signal(barrier, inc=1, device_id=at_tile((t + d) % tiles), device_id_type=MESH)
+        pl.semaphore_signal(barrier, inc=1, device_id=at_tile(t ^ d), device_id_type=MESH)
         return 0
 
     lax.fori_loop(1, n_mem, greet_member, 0)
     lax.fori_loop(1, tiles, greet_tile, 0)
 
-    def row_of(i):
-        return jnp.concatenate([vecs[i, b : b + 1, :] for b in range(obs // LANE)], axis=1)
-
-    observed = row_of(0)
-    noise = row_of(1)
+    def row_of(ref):
+        return jnp.concatenate([ref[b : b + 1, :] for b in range(obs // LANE)], axis=1)
+
+    observed = row_of(observed_in)
+    noise = row_of(noise_in)
     inv_noise = 1.0 / noise
     e_own = observed + jnp.sqrt(noise) * perturb[...]
     e_all[p, 0:mem_local, :] = e_own[:, :obs_half]
@@ -173,8 +206,8 @@
 
     my_edge = pl.multiple_of((1 - la) * (rows - SUB), SUB)
     their_edge = pl.multiple_of(la * (rows + SUB), SUB)
-    lo_w = (lo + n_lon - 1) % n_lon
-    lo_e = (lo + 1) % n_lon
+    lo_w = (lo + n_lon - 1) & (n_lon - 1)
+    lo_e = (lo + 1) & (n_lon - 1)
 
     def halo(i, src, dst, lat, lon):
         return pltpu.make_async_remote_copy(
@@ -192,23 +225,29 @@
     for copy in halos:
         copy.start()
 
+    far = [0]
+
+    def send_far(count):
+        lax.fori_loop(far[0], far[0] + count, start(far_copy), 0)
+        far[0] += count
+
     def e_copy(d):
-        peer = (p + d) % half
+        peer = p ^ d
         return pltpu.make_async_remote_copy(
             src_ref=e_all.at[p], dst_ref=e_all.at[p], send_sem=e_send.at[peer], recv_sem=e_recv.at[p],
             device_id=at_member(zh * half + peer), device_id_type=MESH,
         )
 
     def e_arrival(d):
-        peer = (p + d) % half
+        peer = p ^ d
         return pltpu.make_async_remote_copy(
             src_ref=e_all.at[p], dst_ref=e_all.at[peer], send_sem=e_send.at[peer], recv_sem=e_recv.at[peer],
             device_id=at_member(zh * half + peer), device_id_type=MESH,
         )
 
     def th_copy(d):
-        peer = (m + d) % n_mem
-        r = pl.multiple_of((peer % half) * chunk_rows, chunk_rows)
+        peer = m ^ d
+        r = pl.multiple_of((peer & (half - 1)) * chunk_rows, chunk_rows)
         return pltpu.make_async_remote_copy(
             src_ref=th_own.at[:, :, pl.ds(r, chunk_rows), :],
             dst_ref=th_all.at[:, pl.ds(m * mem_local, mem_local)],
@@ -217,11 +256,32 @@
         )
 
     def th_arrival(d):
-        peer = (m + d) % n_mem
+        peer = m ^ d
         return pltpu.make_async_remote_copy(
             src_ref=th_own.at[:, :, pl.ds(0, chunk_rows), :],
             dst_ref=th_all.at[:, pl.ds(peer * mem_local, mem_local)],
             send_sem=th_send.at[peer], recv_sem=th_recv.at[peer],
+            device_id=at_member(peer), device_id_type=MESH,
+        )
+
+    def far_copy(i):
+        b, d = i // half, half + (i & (half - 1))
+        peer = m ^ d
+        r = pl.multiple_of((peer & (half - 1)) * chunk_rows, chunk_rows)
+        return pltpu.make_async_remote_copy(
+            src_ref=th_own.at[b, :, pl.ds(r, chunk_rows), :],
+            dst_ref=th_all.at[b, pl.ds(m * mem_local, mem_local)],
+            send_sem=f_send.at[i], recv_sem=f_recv.at[i],
+            device_id=at_member(peer), device_id_type=MESH,
+        )
+
+    def far_arrival(i):
+        b, d = i // half, half + (i & (half - 1))
+        peer = m ^ d
+        return pltpu.make_async_remote_copy(
+            src_ref=th_own.at[b, :, pl.ds(0, chunk_rows), :],
+            dst_ref=th_all.at[b, pl.ds(peer * mem_local, mem_local)],
+            send_sem=f_send.at[i], recv_sem=f_recv.at[i],
             device_id=at_member(peer), device_id_type=MESH,
         )
 
@@ -243,8 +303,7 @@
             return 0
         return body
 
-    lax.fori_loop(1, half, start(e_copy), 0)
-    lax.fori_loop(1, n_mem, start(th_copy), 0)
+    lax.fori_loop(1, half, start(th_copy), 0)
     own_chunk = pl.multiple_of(p * chunk_rows, chunk_rows)
     own_th = pltpu.make_async_copy(
         th_own.at[:, :, pl.ds(own_chunk, chunk_rows), :],
@@ -252,9 +311,13 @@
         in_sem.at[3],
     )
     own_th.start()
+    send_far(FAR[0])
 
     for copy in halos:
         copy.wait_recv()
+    lax.fori_loop(1, half, start(e_copy), 0)
+
+    send_far(FAR[1])
 
     for q in range(planes):
         block = lat_in[q]
@@ -295,6 +358,7 @@
         return 0
 
     lax.fori_loop(0, n_chunks, shared, 0)
+    send_far(FAR[2])
 
     def first_step(i, _):
         r = pl.multiple_of(i * SUB, SUB)
@@ -317,6 +381,7 @@
         return 0
 
     lax.fori_loop(0, n_chunks, first_step, 0)
+    send_far(FAR[3])
 
     flat_cells = cells.reshape(rows * blocks * SUB, LANE)
 
@@ -347,6 +412,7 @@
         return 0
 
     lax.fori_loop(1, n_chunks - 1, second_step, 0)
+    send_far(FAR[4])
 
     obs_blocks = obs // LANE
     step_of = 8
@@ -377,22 +443,35 @@
     pred_out[:, obs_half:obs] = own_pred[mem_local:SUB]
 
     def p_copy(d):
-        peer = (m + d) % n_mem
+        peer = m ^ d
         return pltpu.make_async_remote_copy(
             src_ref=pred_all.at[m], dst_ref=pred_all.at[m], send_sem=p_send.at[peer], recv_sem=p_recv.at[m],
             device_id=at_member(peer), device_id_type=MESH,
         )
 
     def p_arrival(d):
-        peer = (m + d) % n_mem
+        peer = m ^ d
         return pltpu.make_async_remote_copy(
             src_ref=pred_all.at[m], dst_ref=pred_all.at[peer], send_sem=p_send.at[peer], recv_sem=p_recv.at[peer],
             device_id=at_member(peer), device_id_type=MESH,
         )
 
-    lax.fori_loop(1, n_mem, start(p_copy), 0)
+    def p_relay(d):
+        far_slot = m ^ half
+        return pltpu.make_async_remote_copy(
+            src_ref=pred_all.at[far_slot], dst_ref=pred_all.at[far_slot],
+            send_sem=p_send.at[far_slot ^ d], recv_sem=p_recv.at[far_slot],
+            device_id=at_member(m ^ d), device_id_type=MESH,
+        )
+
+    p_copy(half).start()
+    lax.fori_loop(1, half, start(p_copy), 0)
     lax.fori_loop(1, half, wait_recv(e_arrival), 0)
-    lax.fori_loop(1, n_mem, wait_recv(p_arrival), 0)
+    p_arrival(half).wait_recv()
+    lax.fori_loop(1, half, start(p_relay), 0)
+    send_far(FAR[5])
+    lax.fori_loop(1, half, wait_recv(p_arrival), 0)
+    lax.fori_loop(half + 1, n_mem, wait_recv(p_arrival), 0)
 
     low = lax.broadcasted_iota(jnp.int32, (SUB, obs_half), 0) < mem_local
 
@@ -432,7 +511,7 @@
     )
 
     def r_copy(d):
-        peer = (t + d) % tiles
+        peer = t ^ d
         return pltpu.make_async_remote_copy(
             src_ref=g_own.at[pl.ds(pl.multiple_of(peer * part, SUB), part), :], dst_ref=rs_in.at[t],
             send_sem=r_send.at[peer], recv_sem=r_recv.at[t],
@@ -440,7 +519,7 @@
         )
 
     def r_arrival(d):
-        peer = (t + d) % tiles
+        peer = t ^ d
         return pltpu.make_async_remote_copy(
             src_ref=g_own.at[pl.ds(0, part), :], dst_ref=rs_in.at[peer],
             send_sem=r_send.at[peer], recv_sem=r_recv.at[peer],
@@ -449,6 +528,7 @@
 
     my_part = pl.multiple_of(t * part, SUB)
     lax.fori_loop(1, tiles, start(r_copy), 0)
+    send_far(FAR[6])
     rs_in[t] = g_own[pl.ds(my_part, part), :]
     lax.fori_loop(1, tiles, wait_recv(r_arrival), 0)
     total_part = rs_in[0]
@@ -457,7 +537,7 @@
     ab[pl.ds(my_part, part), :] = total_part
 
     def a_copy(d):
-        peer = (t + d) % tiles
+        peer = t ^ d
         mine = ab.at[pl.ds(my_part, part), :]
         return pltpu.make_async_remote_copy(
             src_ref=mine, dst_ref=mine, send_sem=a_send.at[peer], recv_sem=a_recv.at[t],
@@ -465,7 +545,7 @@
         )
 
     def a_arrival(d):
-        peer = (t + d) % tiles
+        peer = t ^ d
         return pltpu.make_async_remote_copy(
             src_ref=ab.at[pl.ds(my_part, part), :],
             dst_ref=ab.at[pl.ds(pl.multiple_of(peer * part, SUB), part), :],
@@ -474,14 +554,17 @@
         )
 
     lax.fori_loop(1, tiles, start(a_copy), 0)
+    send_far(FAR[7])
     lax.fori_loop(1, tiles, wait_recv(a_arrival), 0)
 
+    send_far(blocks * half - far[0])
     eye = lax.broadcasted_iota(jnp.int32, (members, members), 0) == lax.broadcasted_iota(
         jnp.int32, (members, members), 1
     )
-    inverse = spd_inverse(ab[0:members, :] + jnp.where(eye, LM, 0.0))
+    mat[...] = ab[0:members, :] + jnp.where(eye, LM, 0.0)
+    invert(mat)
     w = jnp.dot(
-        ab[members : members + half_members, :], inverse, precision=lax.Precision.HIGHEST,
+        ab[members : members + half_members, :], mat[...], precision=lax.Precision.HIGHEST,
         preferred_element_type=F32,
     )
     w = scale * (w - jnp.mean(w, axis=1, keepdims=True))
@@ -492,10 +575,11 @@
     )
 
     own_th.wait()
-    lax.fori_loop(1, n_mem, wait_recv(th_arrival), 0)
+    lax.fori_loop(1, half, wait_recv(th_arrival), 0)
+
 
     def o_copy(b, d):
-        peer = (p + d) % half
+        peer = p ^ d
         return pltpu.make_async_remote_copy(
             src_ref=upd.at[b, pl.ds(peer * mem_local, mem_local)],
             dst_ref=out_hbm.at[:, pl.ds(own_chunk, chunk_rows), pl.ds(b * LANE, LANE)],
@@ -504,7 +588,7 @@
         )
 
     def o_arrival(b, d):
-        peer = (p + d) % half
+        peer = p ^ d
         return pltpu.make_async_remote_copy(
             src_ref=upd.at[b, pl.ds(peer * mem_local, mem_local)],
             dst_ref=out_hbm.at[
@@ -519,6 +603,7 @@
     own_out = []
     for b in range(blocks):
         at_b = b * members * chunk_rows
+        lax.fori_loop(b * half, (b + 1) * half, wait_recv(far_arrival), 0)
         for r in range(0, chunk_rows, 2):
             field = jnp.concatenate(
                 [flat[pl.ds(at_b + r + k, members, stride=chunk_rows), :] for k in range(2)], axis=1
@@ -545,8 +630,10 @@
     for copy in halos:
         copy.wait_send()
     lax.fori_loop(1, half, wait_send(e_copy), 0)
-    lax.fori_loop(1, n_mem, wait_send(th_copy), 0)
-    lax.fori_loop(1, n_mem, wait_send(p_copy), 0)
+    lax.fori_loop(1, half, wait_send(th_copy), 0)
+    lax.fori_loop(0, blocks * half, wait_send(far_copy), 0)
+    lax.fori_loop(1, half + 1, wait_send(p_copy), 0)
+    lax.fori_loop(1, half, wait_send(p_relay), 0)
     lax.fori_loop(1, tiles, wait_send(r_copy), 0)
     lax.fori_loop(1, tiles, wait_send(a_copy), 0)
     for b in range(blocks):
@@ -567,7 +654,7 @@
     planes = mem_local + 6
     pad_rows, pad_cols = rows + 2 * SUB, cols + LANE
     g_rows = members + half_members
-    vecs = jnp.stack([observed.reshape(obs // LANE, LANE), noise_var.reshape(obs // LANE, LANE)])
+    folded = [a.reshape(obs // LANE, LANE) for a in (obs_index, observed, noise_var)]
     dma = pltpu.SemaphoreType.DMA
     theta_new, pred = pl.pallas_call(
         functools.partial(kernel, sizes),
@@ -580,6 +667,7 @@
             pl.BlockSpec(memory_space=pl.ANY),
             pl.BlockSpec(memory_space=pl.ANY),
             pl.BlockSpec(memory_space=pltpu.SMEM),
+            pl.BlockSpec(memory_space=pltpu.VMEM),
             pl.BlockSpec(memory_space=pltpu.VMEM),
             pl.BlockSpec(memory_space=pltpu.VMEM),
             pl.BlockSpec(memory_space=pltpu.VMEM),
@@ -607,10 +695,12 @@
             pltpu.VMEM((g_rows, members), F32),
             pltpu.VMEM((tiles, g_rows // tiles, members), F32),
             pltpu.VMEM((g_rows, members), F32),
+            pltpu.VMEM((members, members), F32),
             pltpu.VMEM((cols // LANE, half_members, chunk_rows, LANE), F32),
             dma((4 + cols // LANE,)),
             dma((5,)), dma((5,)),
             dma((n_mem,)), dma((n_mem,)),
+            dma((cols // LANE * half,)), dma((cols // LANE * half,)),
             dma((half,)), dma((half,)),
             dma((n_mem,)), dma((n_mem,)),
             dma((tiles,)), dma((tiles,)),
@@ -621,7 +711,7 @@
             collective_id=0, has_side_effects=True, vmem_limit_bytes=56 * 1024 * 1024
         ),
         name="inversion",
-    )(theta, tracer, velocity.reshape(4, rows, cols), obs_index, obs_index.reshape(obs // LANE, LANE), vecs, obs_perturb.T)
+    )(theta, tracer, velocity.reshape(4, rows, cols), obs_index, *folded, obs_perturb.T)
     return theta_new, pred.T
 
 

time: 108 us -> 86.4 us (0.80)
  the two profiles are of different devices: /device:TPU:1 before, /device:TPU:227 now
where the time goes in v2:
time: 86.4 us; the launch traced here: 86.2 us
  Pallas kernels  82.9 us (96%)
  local copies, waits for them, and re-layouts  2.68 us (3%)
    pallas_call x1, Pallas kernels, on_device(): pl.pallas_call(functools.partial(kernel, sizes), out_shape=(jax.ShapeDtyp...  82.9 us
    unnamed x4, local copies, waits for them, and re-layouts  2.68 us

profile of v2, /device:TPU:227, one launch (start us, length us, event | category | flops | bytes accessed | tf_op | source)
XLA Modules:
  0.0 86.2 jit_solution(3126342863348297959)
XLA Ops:
  0.6 82.9 %inversion.1 = (f32[4,128,384]{2,1,0:T(8,128)}, f32[4,768]{1,0:T(4,128)}) custom-call(f32[4,128,384]{2,1,0:T(8,128)} %theta_hbm.1, f32[2,128,384]{2,1,0:T(8,128)} %tracer_hbm.1, f32[4,128,384]{2,1,0:T(8,128)} %bitcast.6, s32[768]{0:T(1024)} %obs_index.1, s32[6,128]{1,0:T(8,128)} %bitcast.7, f32[6,128]{1,0:T(8,128)} %bitcast.10, f32[6,128]{1,0:T(8,128)} %bitcast.11, ...), custom_call_target="tpu_custom_call" | custom-call | tf_op jit(solution)/shard_map/inversion/pallas_call | solution.py:659
  83.5 0.0 copy-start
  83.5 2.1 %copy.11 = f32[4,128,384]{2,1,0:T(8,128)} copy(f32[4,128,384]{2,1,0:T(8,128)} %get-tuple-element.8) | data formatting | bytes 1572864
  85.6 0.0 copy-done
  85.6 0.6 copy.12
Async XLA Ops:
  83.5 2.1 %copy-start = (f32[4,768]{1,0:T(4,128)S(1)}, f32[4,768]{1,0:T(4,128)}, u32[]{:S(2)}) copy-start(f32[4,768]{1,0:T(4,128)} %get-tuple-element.5) | copy-start | bytes 36868

commit v3 on v2

--- a/solution.py
+++ b/solution.py
@@ -13,7 +13,7 @@
 BF16 = jnp.bfloat16
 LANE = 128
 SUB = 8
-FAR = (6, 4, 4, 4, 4, 4, 4, 4)
+FAR = (6, 6, 6, 4, 0, 8, 6, 6)
 
 
 def lane_shift(x, by):
@@ -36,6 +36,14 @@
 
     def row(x, r):
         return jnp.broadcast_to(x[r : r + 1, :], shape)
+
+    row_all = lax.broadcasted_iota(jnp.int32, (n, n), 0)
+    lane_all = lax.broadcasted_iota(jnp.int32, (n, n), 1)
+
+    def spread(old, first, panel):
+        wide = jnp.concatenate([panel] * (n // SUB), axis=0)
+        wide = jnp.where((row_all >= first) & (row_all < first + SUB), wide, 0.0)
+        return jnp.dot(old, wide, precision=lax.Precision.HIGHEST, preferred_element_type=F32)
 
     def behind(first, panel):
         lanes = [jnp.full(shape, (first + c) & (n - 1), jnp.int32) for c in range(SUB)]
@@ -80,16 +88,17 @@
                 jnp.where(at0, 0.0, jnp.where(at1, 1.0, row(panel, c + 1))),
                 jnp.where(at0 | at1, 0.0, panel),
             )
-        for i in range(n // SUB):
-            tile = mat[i * SUB : (i + 1) * SUB, :]
-            mat[i * SUB : (i + 1) * SUB, :] = jnp.where(b - 1 == i, tile, update(tile))
+        old = mat[...]
+        kept = (row_all >= first - SUB) & (row_all < first)
+        left = (lane_all >= first - SUB) & (lane_all < first)
+        mat[...] = jnp.where(kept, old, jnp.where(left, 0.0, old) - spread(old, first - SUB, last))
         mat[pl.ds(first, SUB), :] = panel
         return panel
 
     last = lax.fori_loop(0, n // SUB, eliminate_panel, jnp.zeros(shape, F32))
-    update = behind(n - SUB, last)
-    for i in range(n // SUB - 1):
-        mat[i * SUB : (i + 1) * SUB, :] = update(mat[i * SUB : (i + 1) * SUB, :])
+    old = mat[...]
+    done = jnp.where(lane_all >= n - SUB, 0.0, old) - spread(old, n - SUB, last)
+    mat[...] = jnp.where(row_all >= n - SUB, old, done)
 
 
 def kernel(
@@ -115,7 +124,7 @@
     obs = perturb.shape[1]
     obs_half = obs // 2
     g_rows = g_own.shape[0]
-    part = g_rows // tiles
+    part = g_rows // half
     scale = 1.0 / float(members - 1) ** 0.5
 
     m = lax.axis_index("member")
@@ -416,21 +425,29 @@
 
     obs_blocks = obs // LANE
     step_of = 8
+    low8 = sub8 < mem_local
     obs_lane = [
-        jnp.broadcast_to(obs_cell[b : b + 1, :] & (LANE - 1), (SUB, LANE)) for b in range(obs_blocks)
+        jnp.where(
+            low8,
+            jnp.broadcast_to(obs_cell[a : a + 1, :], (SUB, LANE)),
+            jnp.broadcast_to(obs_cell[a + obs_blocks // 2 : a + obs_blocks // 2 + 1, :], (SUB, LANE)),
+        )
+        & (LANE - 1)
+        for a in range(obs_blocks // 2)
     ]
 
     def gather(i, accs):
         accs = list(accs)
         for k in range(step_of):
             s = i * step_of + k
-            for b in range(obs_blocks):
-                block = lax.shift_right_logical(obs_index[b * LANE + s], LANE.bit_length() - 1)
-                got = cells[block]
-                got = jnp.take_along_axis(got, obs_lane[b], axis=1, mode="promise_in_bounds")
-                h = b // (obs_blocks // 2)
-                here = (lane8 == s) & (sub8 // mem_local == h)
-                a = b % (obs_blocks // 2)
+            here = lane8 == s
+            for a in range(obs_blocks // 2):
+                got = [
+                    cells[lax.shift_right_logical(obs_index[b * LANE + s], LANE.bit_length() - 1)]
+                    for b in (a, a + obs_blocks // 2)
+                ]
+                got = jnp.where(low8, got[0], got[1])
+                got = jnp.take_along_axis(got, obs_lane[a], axis=1, mode="promise_in_bounds")
                 accs[a] = jnp.where(here, got, accs[a])
         return tuple(accs)
 
@@ -466,10 +483,10 @@
 
     p_copy(half).start()
     lax.fori_loop(1, half, start(p_copy), 0)
+    send_far(FAR[5])
     lax.fori_loop(1, half, wait_recv(e_arrival), 0)
     p_arrival(half).wait_recv()
     lax.fori_loop(1, half, start(p_relay), 0)
-    send_far(FAR[5])
     lax.fori_loop(1, half, wait_recv(p_arrival), 0)
     lax.fori_loop(half + 1, n_mem, wait_recv(p_arrival), 0)
 
@@ -505,15 +522,18 @@
 
     lax.fori_loop(0, half_members // SUB, innovate, 0)
 
-    g_own[...] = lax.dot_general(
+    g_own[members + half_members :, :] = jnp.zeros((g_rows - members - half_members, members), F32)
+    g_own[0 : members + half_members, :] = lax.dot_general(
         left[...], weighted[...], (((1,), (1,)), ((), ())), precision=lax.Precision.HIGHEST,
         preferred_element_type=F32,
     )
 
+    my_part = pl.multiple_of(p * part, SUB)
+
     def r_copy(d):
         peer = t ^ d
         return pltpu.make_async_remote_copy(
-            src_ref=g_own.at[pl.ds(pl.multiple_of(peer * part, SUB), part), :], dst_ref=rs_in.at[t],
+            src_ref=g_own.at[pl.ds(my_part, part), :], dst_ref=rs_in.at[t],
             send_sem=r_send.at[peer], recv_sem=r_recv.at[t],
             device_id=at_tile(peer), device_id_type=MESH,
         )
@@ -526,7 +546,6 @@
             device_id=at_tile(peer), device_id_type=MESH,
         )
 
-    my_part = pl.multiple_of(t * part, SUB)
     lax.fori_loop(1, tiles, start(r_copy), 0)
     send_far(FAR[6])
     rs_in[t] = g_own[pl.ds(my_part, part), :]
@@ -537,25 +556,25 @@
     ab[pl.ds(my_part, part), :] = total_part
 
     def a_copy(d):
-        peer = t ^ d
+        peer = p ^ d
         mine = ab.at[pl.ds(my_part, part), :]
         return pltpu.make_async_remote_copy(
-            src_ref=mine, dst_ref=mine, send_sem=a_send.at[peer], recv_sem=a_recv.at[t],
-            device_id=at_tile(peer), device_id_type=MESH,
+            src_ref=mine, dst_ref=mine, send_sem=a_send.at[peer], recv_sem=a_recv.at[p],
+            device_id=at_member(zh * half + peer), device_id_type=MESH,
         )
 
     def a_arrival(d):
-        peer = t ^ d
+        peer = p ^ d
         return pltpu.make_async_remote_copy(
             src_ref=ab.at[pl.ds(my_part, part), :],
             dst_ref=ab.at[pl.ds(pl.multiple_of(peer * part, SUB), part), :],
             send_sem=a_send.at[peer], recv_sem=a_recv.at[peer],
-            device_id=at_tile(peer), device_id_type=MESH,
-        )
-
-    lax.fori_loop(1, tiles, start(a_copy), 0)
+            device_id=at_member(zh * half + peer), device_id_type=MESH,
+        )
+
+    lax.fori_loop(1, half, start(a_copy), 0)
     send_far(FAR[7])
-    lax.fori_loop(1, tiles, wait_recv(a_arrival), 0)
+    lax.fori_loop(1, half, wait_recv(a_arrival), 0)
 
     send_far(blocks * half - far[0])
     eye = lax.broadcasted_iota(jnp.int32, (members, members), 0) == lax.broadcasted_iota(
@@ -635,7 +654,7 @@
     lax.fori_loop(1, half + 1, wait_send(p_copy), 0)
     lax.fori_loop(1, half, wait_send(p_relay), 0)
     lax.fori_loop(1, tiles, wait_send(r_copy), 0)
-    lax.fori_loop(1, tiles, wait_send(a_copy), 0)
+    lax.fori_loop(1, half, wait_send(a_copy), 0)
     for b in range(blocks):
         own_out[b].wait()
         lax.fori_loop(1, half, wait_recv(functools.partial(o_arrival, b)), 0)
@@ -653,7 +672,7 @@
     chunk_rows = rows // half
     planes = mem_local + 6
     pad_rows, pad_cols = rows + 2 * SUB, cols + LANE
-    g_rows = members + half_members
+    g_rows = half * SUB * -(-(members + half_members) // (half * SUB))
     folded = [a.reshape(obs // LANE, LANE) for a in (obs_index, observed, noise_var)]
     dma = pltpu.SemaphoreType.DMA
     theta_new, pred = pl.pallas_call(
@@ -691,9 +710,9 @@
             pltpu.VMEM((n_mem, SUB, obs // 2), F32),
             pltpu.VMEM((members, obs), F32),
             pltpu.VMEM((members, obs), F32),
-            pltpu.VMEM((g_rows, obs), F32),
+            pltpu.VMEM((members + half_members, obs), F32),
             pltpu.VMEM((g_rows, members), F32),
-            pltpu.VMEM((tiles, g_rows // tiles, members), F32),
+            pltpu.VMEM((tiles, g_rows // half, members), F32),
             pltpu.VMEM((g_rows, members), F32),
             pltpu.VMEM((members, members), F32),
             pltpu.VMEM((cols // LANE, half_members, chunk_rows, LANE), F32),
@@ -704,7 +723,7 @@
             dma((half,)), dma((half,)),
             dma((n_mem,)), dma((n_mem,)),
             dma((tiles,)), dma((tiles,)),
-            dma((tiles,)), dma((tiles,)),
+            dma((half,)), dma((half,)),
             dma((cols // LANE, half)), dma((cols // LANE, half)),
         ],
         compiler_params=pltpu.CompilerParams(

time: 86.4 us -> 79.9 us (0.925)
  the two profiles are of different devices: /device:TPU:227 before, /device:TPU:1 now
where the time goes in v3:
time: 79.9 us; the launch traced here: 79.7 us
  Pallas kernels  76.4 us (96%)
  local copies, waits for them, and re-layouts  2.68 us (3%)
    pallas_call x1, Pallas kernels, on_device(): pl.pallas_call(functools.partial(kernel, sizes), out_shape=(jax.ShapeDtyp...  76.4 us
    unnamed x4, local copies, waits for them, and re-layouts  2.68 us

profile of v3, /device:TPU:1, one launch (start us, length us, event | category | flops | bytes accessed | tf_op | source)
XLA Modules:
  0.0 79.7 jit_solution(11689637256601747628)
XLA Ops:
  0.6 76.4 %inversion.1 = (f32[4,128,384]{2,1,0:T(8,128)}, f32[4,768]{1,0:T(4,128)}) custom-call(f32[4,128,384]{2,1,0:T(8,128)} %theta_hbm.1, f32[2,128,384]{2,1,0:T(8,128)} %tracer_hbm.1, f32[4,128,384]{2,1,0:T(8,128)} %bitcast.6, s32[768]{0:T(1024)} %obs_index.1, s32[6,128]{1,0:T(8,128)} %bitcast.7, f32[6,128]{1,0:T(8,128)} %bitcast.10, f32[6,128]{1,0:T(8,128)} %bitcast.11, ...), custom_call_target="tpu_custom_call" | custom-call | tf_op jit(solution)/shard_map/inversion/pallas_call | solution.py:678
  77.0 0.0 copy-start
  77.0 2.1 %copy.11 = f32[4,128,384]{2,1,0:T(8,128)} copy(f32[4,128,384]{2,1,0:T(8,128)} %get-tuple-element.8) | data formatting | bytes 1572864
  79.1 0.0 copy-done
  79.1 0.6 copy.12
Async XLA Ops:
  77.0 2.1 %copy-start = (f32[4,768]{1,0:T(4,128)S(1)}, f32[4,768]{1,0:T(4,128)}, u32[]{:S(2)}) copy-start(f32[4,768]{1,0:T(4,128)} %get-tuple-element.5) | copy-start | bytes 36868

commit v4 on v3

--- a/solution.py
+++ b/solution.py
@@ -103,12 +103,12 @@
 
 def kernel(
     sizes,
-    theta_hbm, tracer_hbm, velocity_hbm, obs_index, obs_cell, observed_in, noise_in, perturb,
+    theta_hbm, tracer_hbm, velocity_hbm, obs_index, obs_cell_hbm, observed_hbm, noise_hbm, perturb_hbm,
     out_hbm, pred_out,
-    th_own, x, lat_in, east_out, west_out, east_in, west_in,
+    obs_cell, observed_in, noise_in, perturb, th_own, x, lat_in, east_out, west_out, east_in, west_in,
     base, diffs, faces, c1, cells,
     th_all, e_all, pred_all, pred_mat, weighted, left, g_own, rs_in, ab, mat, upd,
-    in_sem, halo_send, halo_recv, th_send, th_recv, f_send, f_recv, e_send, e_recv, p_send, p_recv,
+    in_sem, small_sem, halo_send, halo_recv, th_send, th_recv, f_send, f_recv, e_send, e_recv, p_send, p_recv,
     r_send, r_recv, a_send, a_recv, o_send, o_recv,
 ):
     n_mem, n_lat, n_lon = sizes
@@ -140,6 +140,19 @@
     def at_tile(peer):
         return {"member": m, "lat": lax.shift_right_logical(peer, n_lon.bit_length() - 1), "lon": peer & (n_lon - 1)}
 
+    barrier = pltpu.get_barrier_semaphore()
+
+    def greet_member(d, _):
+        pl.semaphore_signal(barrier, inc=1, device_id=at_member(m ^ d), device_id_type=MESH)
+        return 0
+
+    def greet_tile(d, _):
+        pl.semaphore_signal(barrier, inc=1, device_id=at_tile(t ^ d), device_id_type=MESH)
+        return 0
+
+    lax.fori_loop(1, n_mem, greet_member, 0)
+    lax.fori_loop(1, tiles, greet_tile, 0)
+
     loads = [
         pltpu.make_async_copy(theta_hbm.at[:, :, pl.ds(b * LANE, LANE)], th_own.at[b], in_sem.at[4 + b])
         for b in range(blocks)
@@ -151,31 +164,14 @@
             velocity_hbm, x.at[pl.ds(mem_local + 2, 4), pl.ds(SUB, rows), pl.ds(0, cols)], in_sem.at[2]
         ),
     ]
-    for load in loads:
+    smalls = [
+        pltpu.make_async_copy(src, dst, small_sem.at[i])
+        for i, (src, dst) in enumerate(
+            ((obs_cell_hbm, obs_cell), (observed_hbm, observed_in), (noise_hbm, noise_in), (perturb_hbm, perturb))
+        )
+    ]
+    for load in loads + smalls:
         load.start()
-
-    barrier = pltpu.get_barrier_semaphore()
-
-    def greet_member(d, _):
-        pl.semaphore_signal(barrier, inc=1, device_id=at_member(m ^ d), device_id_type=MESH)
-        return 0
-
-    def greet_tile(d, _):
-        pl.semaphore_signal(barrier, inc=1, device_id=at_tile(t ^ d), device_id_type=MESH)
-        return 0
-
-    lax.fori_loop(1, n_mem, greet_member, 0)
-    lax.fori_loop(1, tiles, greet_tile, 0)
-
-    def row_of(ref):
-        return jnp.concatenate([ref[b : b + 1, :] for b in range(obs // LANE)], axis=1)
-
-    observed = row_of(observed_in)
-    noise = row_of(noise_in)
-    inv_noise = 1.0 / noise
-    e_own = observed + jnp.sqrt(noise) * perturb[...]
-    e_all[p, 0:mem_local, :] = e_own[:, :obs_half]
-    e_all[p, mem_local:SUB, :] = e_own[:, obs_half:]
 
     for load in loads[:blocks]:
         load.wait()
@@ -321,6 +317,19 @@
     )
     own_th.start()
     send_far(FAR[0])
+
+    for load in smalls:
+        load.wait()
+
+    def row_of(ref):
+        return jnp.concatenate([ref[b : b + 1, :] for b in range(obs // LANE)], axis=1)
+
+    observed = row_of(observed_in)
+    noise = row_of(noise_in)
+    inv_noise = 1.0 / noise
+    e_own = observed + jnp.sqrt(noise) * perturb[...]
+    e_all[p, 0:mem_local, :] = e_own[:, :obs_half]
+    e_all[p, mem_local:SUB, :] = e_own[:, obs_half:]
 
     for copy in halos:
         copy.wait_recv()
@@ -678,21 +687,25 @@
     theta_new, pred = pl.pallas_call(
         functools.partial(kernel, sizes),
         out_shape=(
-            jax.ShapeDtypeStruct(theta.shape, F32),
-            jax.ShapeDtypeStruct((mem_local, obs), F32),
+            pltpu.VMEM(theta.shape, F32),
+            pltpu.VMEM((mem_local, obs), F32),
         ),
         in_specs=[
             pl.BlockSpec(memory_space=pl.ANY),
             pl.BlockSpec(memory_space=pl.ANY),
             pl.BlockSpec(memory_space=pl.ANY),
             pl.BlockSpec(memory_space=pltpu.SMEM),
-            pl.BlockSpec(memory_space=pltpu.VMEM),
-            pl.BlockSpec(memory_space=pltpu.VMEM),
-            pl.BlockSpec(memory_space=pltpu.VMEM),
-            pl.BlockSpec(memory_space=pltpu.VMEM),
+            pl.BlockSpec(memory_space=pl.ANY),
+            pl.BlockSpec(memory_space=pl.ANY),
+            pl.BlockSpec(memory_space=pl.ANY),
+            pl.BlockSpec(memory_space=pl.ANY),
         ],
         out_specs=(pl.BlockSpec(memory_space=pl.ANY), pl.BlockSpec(memory_space=pltpu.VMEM)),
         scratch_shapes=[
+            pltpu.VMEM((obs // LANE, LANE), jnp.int32),
+            pltpu.VMEM((obs // LANE, LANE), F32),
+            pltpu.VMEM((obs // LANE, LANE), F32),
+            pltpu.VMEM((mem_local, obs), F32),
             pltpu.VMEM((cols // LANE, mem_local, rows, LANE), F32),
             pltpu.VMEM((planes, pad_rows, pad_cols), F32),
             pltpu.VMEM((planes, SUB, cols), F32),
@@ -717,6 +730,7 @@
             pltpu.VMEM((members, members), F32),
             pltpu.VMEM((cols // LANE, half_members, chunk_rows, LANE), F32),
             dma((4 + cols // LANE,)),
+            dma((4,)),
             dma((5,)), dma((5,)),
             dma((n_mem,)), dma((n_mem,)),
             dma((cols // LANE * half,)), dma((cols // LANE * half,)),

time: 79.9 us -> 77.6 us (0.971)
  Pallas kernels: 76.4 us -> 75.2 us
  local copies, waits for them, and re-layouts: 2.68 us -> 1.48 us
    pallas_call x1, Pallas kernels: 76.4 us -> 75.2 us  [on_device(): pl.pallas_call(functools.partial(kernel, sizes), out_shape=(pltpu.VMEM(th...]
    unnamed x4 -> x2, local copies, waits for them, and re-layouts: 2.68 us -> 1.48 us
where the time goes in v4:
time: 77.6 us; the launch traced here: 77.3 us
  Pallas kernels  75.2 us (97%)
  local copies, waits for them, and re-layouts  1.48 us (2%)
    pallas_call x1, Pallas kernels, on_device(): pl.pallas_call(functools.partial(kernel, sizes), out_shape=(pltpu.VMEM(th...  75.2 us

profile of v4, /device:TPU:1, one launch (start us, length us, event | category | flops | bytes accessed | tf_op | source)
XLA Modules:
  0.0 77.3 jit_solution(17074151623177251892)
XLA Ops:
  0.6 75.2 %inversion.1 = (f32[4,128,384]{2,1,0:T(8,128)S(1)}, f32[4,768]{1,0:T(4,128)S(1)}) custom-call(f32[4,128,384]{2,1,0:T(8,128)} %theta_hbm.1, f32[2,128,384]{2,1,0:T(8,128)} %tracer_hbm.1, f32[4,128,384]{2,1,0:T(8,128)} %bitcast.7, s32[768]{0:T(1024)} %obs_index.1, s32[6,128]{1,0:T(8,128)} %bitcast.8, f32[6,128]{1,0:T(8,128)} %bitcast.10, f32[6,128]{1,0:T(8,128)} %bitcast.11, ...), custom_call_target="tpu_custom_call" | custom-call | tf_op jit(solution)/shard_map/inversion/pallas_call | solution.py:687
  75.8 0.9 %copy.11 = f32[4,128,384]{2,1,0:T(8,128)} copy(f32[4,128,384]{2,1,0:T(8,128)S(1)} %get-tuple-element.6) | data formatting | bytes 1572864
  76.7 0.6 copy.12

commit v5 on v4

--- a/solution.py
+++ b/solution.py
@@ -105,7 +105,7 @@
     sizes,
     theta_hbm, tracer_hbm, velocity_hbm, obs_index, obs_cell_hbm, observed_hbm, noise_hbm, perturb_hbm,
     out_hbm, pred_out,
-    obs_cell, observed_in, noise_in, perturb, th_own, x, lat_in, east_out, west_out, east_in, west_in,
+    obs_cell, observed_in, noise_in, perturb, th_own, x, lat_in, east_out, west_out, east_in, west_in, east_rows, west_rows, east_got, west_got,
     base, diffs, faces, c1, cells,
     th_all, e_all, pred_all, pred_mat, weighted, left, g_own, rs_in, ab, mat, upd,
     in_sem, small_sem, halo_send, halo_recv, th_send, th_recv, f_send, f_recv, e_send, e_recv, p_send, p_recv,
@@ -207,6 +207,10 @@
 
     lax.fori_loop(0, rows // SUB, pack, 0)
 
+    kept = east_rows.shape[0]
+    east_rows[...] = jnp.transpose(east_out[...])[0:kept]
+    west_rows[...] = jnp.transpose(west_out[...])[LANE - kept :]
+
     pl.semaphore_wait(barrier, n_mem - 1 + tiles - 1)
 
     my_edge = pl.multiple_of((1 - la) * (rows - SUB), SUB)
@@ -221,8 +225,8 @@
         )
 
     halos = [
-        halo(0, east_out, east_in.at[pl.ds(SUB, rows), :], la, lo_w),
-        halo(1, west_out, west_in.at[pl.ds(SUB, rows), :], la, lo_e),
+        halo(0, east_rows, east_got, la, lo_w),
+        halo(1, west_rows, west_got, la, lo_e),
         halo(2, east_out.at[pl.ds(my_edge, SUB), :], east_in.at[pl.ds(their_edge, SUB), :], 1 - la, lo_w),
         halo(3, west_out.at[pl.ds(my_edge, SUB), :], west_in.at[pl.ds(their_edge, SUB), :], 1 - la, lo_e),
         halo(4, x.at[:, pl.ds(my_edge + SUB, SUB), pl.ds(0, cols)], lat_in, 1 - la, lo),
@@ -336,6 +340,10 @@
     lax.fori_loop(1, half, start(e_copy), 0)
 
     send_far(FAR[1])
+
+    unused = jnp.zeros((LANE - kept, rows), F32)
+    east_in[pl.ds(SUB, rows), :] = jnp.transpose(jnp.concatenate([east_got[...], unused], axis=0))
+    west_in[pl.ds(SUB, rows), :] = jnp.transpose(jnp.concatenate([unused, west_got[...]], axis=0))
 
     for q in range(planes):
         block = lat_in[q]
@@ -713,6 +721,10 @@
             pltpu.VMEM((rows, LANE), F32),
             pltpu.VMEM((pad_rows, LANE), F32),
             pltpu.VMEM((pad_rows, LANE), F32),
+            pltpu.VMEM((SUB * -(-2 * planes // SUB), rows), F32),
+            pltpu.VMEM((SUB * -(-2 * planes // SUB), rows), F32),
+            pltpu.VMEM((SUB * -(-2 * planes // SUB), rows), F32),
+            pltpu.VMEM((SUB * -(-2 * planes // SUB), rows), F32),
             pltpu.VMEM((2, pad_rows, pad_cols), F32),
             pltpu.VMEM((2, 4, pad_rows, pad_cols), F32),
             pltpu.VMEM((mem_local, 4, pad_rows, pad_cols), F32),

time: 77.6 us -> 76.6 us (0.987)
  Pallas kernels: 75.2 us -> 74.2 us
    pallas_call x1, Pallas kernels: 75.2 us -> 74.2 us  [on_device(): pl.pallas_call(functools.partial(kernel, sizes), out_shape=(pltpu.VMEM(th...]
where the time goes in v5:
time: 76.6 us; the launch traced here: 76.3 us
  Pallas kernels  74.2 us (97%)
  local copies, waits for them, and re-layouts  1.48 us (2%)
    pallas_call x1, Pallas kernels, on_device(): pl.pallas_call(functools.partial(kernel, sizes), out_shape=(pltpu.VMEM(th...  74.2 us

profile of v5, /device:TPU:1, one launch (start us, length us, event | category | flops | bytes accessed | tf_op | source)
XLA Modules:
  0.0 76.3 jit_solution(13094951780739433107)
XLA Ops:
  0.6 74.2 %inversion.1 = (f32[4,128,384]{2,1,0:T(8,128)S(1)}, f32[4,768]{1,0:T(4,128)S(1)}) custom-call(f32[4,128,384]{2,1,0:T(8,128)} %theta_hbm.1, f32[2,128,384]{2,1,0:T(8,128)} %tracer_hbm.1, f32[4,128,384]{2,1,0:T(8,128)} %bitcast.7, s32[768]{0:T(1024)} %obs_index.1, s32[6,128]{1,0:T(8,128)} %bitcast.8, f32[6,128]{1,0:T(8,128)} %bitcast.10, f32[6,128]{1,0:T(8,128)} %bitcast.11, ...), custom_call_target="tpu_custom_call" | custom-call | tf_op jit(solution)/shard_map/inversion/pallas_call | solution.py:695
  74.9 0.9 %copy.11 = f32[4,128,384]{2,1,0:T(8,128)} copy(f32[4,128,384]{2,1,0:T(8,128)S(1)} %get-tuple-element.6) | data formatting | bytes 1572864
  75.7 0.6 copy.12
